TPU v7x, 128 devices: a whole 4x4x4 slice. The times are simulated.
128 devices in a mesh: dp: 16 (over x, z_lo, core), expert: 8 (over z_hi, y).
Axes of the slice: x: 4, y: 4, z: 4 (z_hi: 2, z_lo: 2; z = z_hi * 2 + z_lo), core: 2. Of those that a mesh axis runs over, the one named last changes fastest.
Arguments:
- tokens: bfloat16 [1024, 256, 1280], P(('dp', 'expert')), may hold values from -80 to 80
- router: bfloat16 [1280, 16], replicated, may hold values from -1 to 1
- weight_in: bfloat16 [16, 1280, 5120], P('expert', None, 'dp'), may hold values from -0.15625 to 0.15625
- weight_out: bfloat16 [16, 5120, 1280], P('expert', 'dp'), may hold values from -0.078125 to 0.078125
- out_grad: bfloat16 [1024, 256, 1280], P(('dp', 'expert')), may hold values from -6 to 6
Outputs:
- token_grad: bfloat16 [1024, 256, 1280], P(('dp', 'expert'))
- router_grad: float32 [1280, 16], replicated
- weight_in_grad: bfloat16 [16, 1280, 5120], P('expert', None, 'dp')
- weight_out_grad: bfloat16 [16, 5120, 1280], P('expert', 'dp')
All inputs are finite; a program needn't handle non-finite values.
Results may differ from a plain program's by a relative error of at most 0.03.
Values may be sent and summed in bfloat16 or wider, within the bound.
A program may use at most 128 MiB of HBM per device.

v0:
```python
import jax
import jax.numpy as jnp
from jax import lax
from jax.sharding import PartitionSpec as P

root_half = 0.7071067811865476
inv_root_tau = 0.3989422804014327


def gelu_value(hidden):
    return 0.5 * hidden * (1.0 + jax.scipy.special.erf(hidden * root_half))


def gelu_slope(hidden):
    return (
        0.5 * (1.0 + jax.scipy.special.erf(hidden * root_half))
        + hidden * jnp.exp(-0.5 * hidden * hidden) * inv_root_tau
    )


def shards(tokens, router, weight_in, weight_out, out_grad):
    logits = jnp.einsum("bmd,ds->bsm", tokens, router, preferred_element_type=jnp.float32)
    dispatch = jax.nn.softmax(logits, axis=-1)
    combine = jax.nn.softmax(logits, axis=1)
    dispatch_half = dispatch.astype(jnp.bfloat16)
    combine_half = combine.astype(jnp.bfloat16)
    slot_in = jnp.einsum(
        "bsm,bmd->bsd", dispatch_half, tokens, preferred_element_type=jnp.float32
    ).astype(jnp.bfloat16)
    slot_grad = jnp.einsum(
        "bsm,bmd->bsd", combine_half, out_grad, preferred_element_type=jnp.float32
    ).astype(jnp.bfloat16)
    moved_in, moved_grad = (
        lax.all_to_all(slot_in, "expert", split_axis=1, concat_axis=0, tiled=True),
        lax.all_to_all(slot_grad, "expert", split_axis=1, concat_axis=0, tiled=True),
    )
    rows_in, rows_grad = (
        lax.all_gather(moved_in, "dp", axis=0, tiled=True),
        lax.all_gather(moved_grad, "dp", axis=0, tiled=True),
    )
    hidden = jnp.einsum("rjd,jdf->rjf", rows_in, weight_in, preferred_element_type=jnp.float32)
    active = gelu_value(hidden).astype(jnp.bfloat16)
    part_out = jnp.einsum("rjf,jfd->rjd", active, weight_out, preferred_element_type=jnp.float32)
    grad_act = jnp.einsum("rjd,jfd->rjf", rows_grad, weight_out, preferred_element_type=jnp.float32)
    grad_hidden = (grad_act * gelu_slope(hidden)).astype(jnp.bfloat16)
    weight_out_grad = jnp.einsum(
        "rjf,rjd->jfd", active, rows_grad, preferred_element_type=jnp.float32
    ).astype(jnp.bfloat16)
    weight_in_grad = jnp.einsum(
        "rjd,rjf->jdf", rows_in, grad_hidden, preferred_element_type=jnp.float32
    ).astype(jnp.bfloat16)
    part_in = jnp.einsum("rjf,jdf->rjd", grad_hidden, weight_in, preferred_element_type=jnp.float32)
    summed_out, summed_in = (
        lax.psum_scatter(
            part_out.astype(jnp.bfloat16), "dp", scatter_dimension=0, tiled=True
        ).astype(jnp.float32),
        lax.psum_scatter(
            part_in.astype(jnp.bfloat16), "dp", scatter_dimension=0, tiled=True
        ).astype(jnp.float32),
    )
    slot_out, slot_back = (
        lax.all_to_all(
            summed_out.astype(jnp.bfloat16), "expert", split_axis=0, concat_axis=1, tiled=True
        ),
        lax.all_to_all(
            summed_in.astype(jnp.bfloat16), "expert", split_axis=0, concat_axis=1, tiled=True
        ),
    )
    grad_comb = jnp.einsum("bmd,bsd->bsm", out_grad, slot_out, preferred_element_type=jnp.float32)
    comb_logit = combine * (grad_comb - jnp.sum(combine * grad_comb, axis=1, keepdims=True))
    grad_disp = jnp.einsum("bmd,bsd->bsm", tokens, slot_back, preferred_element_type=jnp.float32)
    disp_logit = dispatch * (grad_disp - jnp.sum(dispatch * grad_disp, axis=-1, keepdims=True))
    logit_grad = (comb_logit + disp_logit).astype(jnp.bfloat16)
    token_part = jnp.einsum(
        "bsm,bsd->bmd", dispatch_half, slot_back, preferred_element_type=jnp.float32
    )
    token_part = token_part + jnp.einsum(
        "bsm,ds->bmd", logit_grad, router, preferred_element_type=jnp.float32
    )
    token_grad = token_part.astype(jnp.bfloat16)
    router_term = jnp.einsum("bmd,bsm->ds", tokens, logit_grad, preferred_element_type=jnp.float32)
    router_grad = lax.psum(router_term, ("dp", "expert"))
    return (token_grad, router_grad, weight_in_grad, weight_out_grad)


def solution(mesh):
    in_specs = (
        P(("dp", "expert"), None, None),
        P(),
        P("expert", None, "dp"),
        P("expert", "dp", None),
        P(("dp", "expert"), None, None),
    )
    out_specs = (
        P(("dp", "expert"), None, None),
        P(),
        P("expert", None, "dp"),
        P("expert", "dp", None),
    )
    return jax.shard_map(shards, mesh=mesh, in_specs=in_specs, out_specs=out_specs, check_vma=False)
```

profile of v0, /device:TPU:1, one launch (start us, length us, event | category | flops | bytes accessed | tf_op | source)
XLA Modules:
  0.0 447.7 jit_solution(10608600099201353754)
XLA Ops:
  7.2 4.1 convolution_bitcast_fusion.1
  11.3 1.3 fusion.39
  12.6 3.4 convolution_convert_fusion.4
  16.1 16.4 %all_to_all.72 = bf16[8,16,1280]{2,0,1:T(8,128)(2,1)S(1)} all-to-all(bf16[8,16,1280]{2,0,1:T(8,128)(2,1)S(1)} %copy.15), channel_id=1, replica_groups=mesh['dp'=16,'expert'=8] {'expert'}, dimensions={1} | all-to-all | bytes 655360 | tf_op jit(solution)/shard_map/all_to_all | solution.py:34
  32.5 0.7 copy.27
  33.3 0.6 fusion.40
  33.9 3.3 convolution_convert_fusion.5
  37.3 10.8 %all_to_all.73 = bf16[8,16,1280]{2,0,1:T(8,128)(2,1)S(1)} all-to-all(bf16[8,16,1280]{2,0,1:T(8,128)(2,1)S(1)} %copy.13), channel_id=1, replica_groups=mesh['dp'=16,'expert'=8] {'expert'}, dimensions={1} | all-to-all | bytes 655360 | tf_op jit(solution)/shard_map/all_to_all | solution.py:35
  48.1 0.8 copy.28
  48.9 25.7 %all-gather.5.cloned.1.call-done = bf16[1024,2,1280]{2,0,1:T(8,128)(2,1)} async-done(((bf16[64,2,1280]{2,0,1:T(8,128)(2,1)}), bf16[1024,2,1280]{2,0,1:T(8,128)(2,1)}) %all-gather.5.cloned.1.call-update) | async-done | bytes 5242896 | tf_op jit(solution)/shard_map/all_gather | solution.py:38
  74.6 7.5 %fusion.15 = (bf16[1024,2,320]{0,2,1:T(8,128)(2,1)}, f32[2,1024,320]{1,2,0:T(8,128)}) fusion(bf16[1024,2,1280]{2,0,1:T(8,128)(2,1)} %all-gather.5.cloned.1.call-done, bf16[2,1280,320]{1,2,0:T(8,128)(2,1)S(1)} %copy-done), kind=kOutput, calls=%fused_computation.23 | convolution fusion | flops 1680998400 | bytes 10813440 | tf_op jit(solution)/shard_map/rjd,jdf->rjf/dot_general | solution.py:41
  82.2 32.9 %all-gather.3.cloned.1.call-done = bf16[1024,2,1280]{2,0,1:T(8,128)(2,1)} async-done(((bf16[64,2,1280]{2,0,1:T(8,128)(2,1)}), bf16[1024,2,1280]{2,0,1:T(8,128)(2,1)}) %all-gather.3.cloned.1.call-update) | async-done | bytes 5242896 | tf_op jit(solution)/shard_map/all_gather | solution.py:39
  115.1 5.9 %fusion.11 = bf16[1024,2,320]{0,2,1:T(8,128)(2,1)S(1)} fusion(f32[2,1024,320]{1,2,0:T(8,128)} %get-tuple-element.7, bf16[1024,2,1280]{2,0,1:T(8,128)(2,1)} %all-gather.3.cloned.1.call-done, bf16[2,320,1280]{2,1,0:T(8,128)(2,1)} %param.8), kind=kOutput, calls=%fused_computation.17 | convolution fusion | flops 1684275200 | bytes 10813440 | tf_op jit(solution)/shard_map/rjd,jfd->rjf/dot_general | solution.py:44
  121.0 1.0 copy-done.2
  122.1 4.6 %fusion.4 = bf16[1024,2,1280]{2,0,1:T(8,128)(2,1)} fusion(bf16[1024,2,320]{0,2,1:T(8,128)(2,1)S(1)} %fusion.11, bf16[2,1280,320]{1,2,0:T(8,128)(2,1)S(1)} %copy-done), kind=kOutput, calls=%fused_computation.7 | convolution fusion | flops 1680343040 | bytes 8192000 | tf_op jit(solution)/shard_map/rjf,jdf->rjd/dot_general | solution.py:52
  126.8 7.1 %fusion.5 = bf16[1024,2,1280]{2,0,1:T(8,128)(2,1)} fusion(bf16[1024,2,320]{0,2,1:T(8,128)(2,1)} %get-tuple-element.6, bf16[2,320,1280]{2,1,0:T(8,128)(2,1)} %param.8), kind=kOutput, calls=%fused_computation.8 | convolution fusion | flops 1680343040 | bytes 8192000 | tf_op jit(solution)/shard_map/rjf,jfd->rjd/dot_general | solution.py:43
  133.9 6.2 %convolution_convert_fusion.3 = bf16[2,320,1280]{2,1,0:T(8,128)(2,1)} fusion(bf16[1024,2,320]{0,2,1:T(8,128)(2,1)} %get-tuple-element.6, bf16[1024,2,1280]{2,0,1:T(8,128)(2,1)} %all-gather.3.cloned.1.call-done), kind=kOutput, calls=%fused_computation.11 | convolution fusion | flops 1678540800 | bytes 8192000 | tf_op jit(solution)/shard_map/rjf,rjd->jfd/dot_general | solution.py:46
  140.1 56.5 %reduce-scatter.3.cloned.1.call-done = bf16[64,2,1280]{2,0,1:T(8,128)(2,1)} async-done(((bf16[1024,2,1280]{2,0,1:T(8,128)(2,1)}), bf16[64,2,1280]{2,0,1:T(8,128)(2,1)}) %reduce-scatter.3.cloned.1.call-update) | async-done | bytes 327696 | tf_op jit(solution)/shard_map/reduce_scatter | solution.py:57
  196.6 2.0 copy.17
  198.7 4.8 %all-to-all-start.2 = ((bf16[64,2,1280]{2,1,0:T(2,128)(2,1)}), bf16[64,2,1280]{2,1,0:T(2,128)(2,1)S(1)}, u32[]{:S(2)}, u32[]{:S(2)}) async-start(bf16[64,2,1280]{2,1,0:T(2,128)(2,1)} %copy.17), calls=%async_computation.3 | async-start | bytes 655360 | tf_op jit(solution)/shard_map/all_to_all | solution.py:65
  203.4 5.9 %convolution_convert_fusion.2 = bf16[2,1280,320]{1,2,0:T(8,128)(2,1)} fusion(bf16[1024,2,320]{0,2,1:T(8,128)(2,1)} %copy-done.2, bf16[1024,2,1280]{2,0,1:T(8,128)(2,1)} %all-gather.5.cloned.1.call-done), kind=kOutput, calls=%fused_computation.10 | convolution fusion | flops 1678540800 | bytes 8192000 | tf_op jit(solution)/shard_map/rjd,rjf->jdf/dot_general | solution.py:49
  209.3 60.3 %reduce-scatter.5.cloned.1.call-done = bf16[64,2,1280]{2,0,1:T(8,128)(2,1)} async-done(((bf16[1024,2,1280]{2,0,1:T(8,128)(2,1)}), bf16[64,2,1280]{2,0,1:T(8,128)(2,1)}) %reduce-scatter.5.cloned.1.call-update) | async-done | bytes 327696 | tf_op jit(solution)/shard_map/reduce_scatter | solution.py:54
  269.6 2.0 copy.19
  271.7 6.9 %all-to-all-start.3 = ((bf16[64,2,1280]{2,1,0:T(2,128)(2,1)}), bf16[64,2,1280]{2,1,0:T(2,128)(2,1)S(1)}, u32[]{:S(2)}, u32[]{:S(2)}) async-start(bf16[64,2,1280]{2,1,0:T(2,128)(2,1)} %copy.19), calls=%async_computation.5 | async-start | bytes 655360 | tf_op jit(solution)/shard_map/all_to_all | solution.py:62
  278.9 3.9 fusion.43
  282.9 5.3 %all-to-all-done.3 = bf16[64,2,1280]{2,1,0:T(2,128)(2,1)S(1)} async-done(((bf16[64,2,1280]{2,1,0:T(2,128)(2,1)}), bf16[64,2,1280]{2,1,0:T(2,128)(2,1)S(1)}, u32[]{:S(2)}, u32[]{:S(2)}) %all-to-all-start.3) | async-done | bytes 327712 | tf_op jit(solution)/shard_map/all_to_all | solution.py:62
  288.5 6.9 %fusion.24 = f32[8,16,256]{2,1,0:T(8,128)S(1)} fusion(f32[8,16,256]{2,1,0:T(8,128)S(1)} %get-tuple-element.9, f32[8,256]{1,0:T(8,128)S(1)} %get-tuple-element.8, bf16[8,16,1280]{2,1,0:T(8,128)(2,1)S(1)} %all_to_all.67, bf16[8,256,1280]{2,1,0:T(8,128)(2,1)} %param.9), kind=kOutput, calls=%fused_computation.36 | convolution fusion | flops 167938064 | bytes 5840896 | tf_op jit(solution)/shard_map/sub | solution.py:70
  295.4 4.1 convolution_bitcast_fusion
  299.5 5.9 %fusion.26 = f32[8,256,1280]{2,1,0:T(8,128)} fusion(f32[8,16,256]{2,1,0:T(8,128)S(1)} %fusion.24, f32[8,16,256]{2,1,0:T(8,128)S(1)} %fusion.43, bf16[1280,16]{0,1:T(8,128)(2,1)S(1)} %copy-done.1, f32[8,16,256]{2,1,0:T(8,128)S(1)} %get-tuple-element.5, f32[8,16]{1,0:T(8,128)S(1)} %get-tuple-element.4), kind=kOutput, calls=%fused_computation.38 | convolution fusion | flops 84115840 | bytes 10920448 | tf_op jit(solution)/shard_map/bsm,ds->bmd/dot_general | solution.py:77
  305.4 6.8 %add_convert_fusion = bf16[8,256,1280]{2,1,0:T(8,128)(2,1)} fusion(f32[8,256,1280]{2,1,0:T(8,128)} %fusion.26, bf16[8,16,1280]{2,1,0:T(8,128)(2,1)S(1)} %all_to_all.63, f32[8,16]{1,0:T(8,128)S(1)} %get-tuple-element.4, f32[8,16,256]{2,1,0:T(8,128)S(1)} %convolution_bitcast_fusion.1), kind=kOutput, calls=%fused_computation.4 | convolution fusion | flops 89227648 | bytes 16187904 | tf_op jit(solution)/shard_map/bsm,bsd->bmd/dot_general | solution.py:74
  312.2 127.5 %all-reduce.2.cloned.1.call-done = f32[1280,16]{0,1:T(8,128)} async-done(((f32[1280,16]{0,1:T(8,128)}), f32[1280,16]{0,1:T(8,128)}) %all-reduce.2.cloned.1.call-update) | async-done | bytes 81936 | tf_op jit(solution)/shard_map/psum | solution.py:82
  439.7 1.5 copy.30
  (22 shorter events, 1.2 us)
Async XLA Ops:
  7.2 67.5 %copy-start = (bf16[2,1280,320]{1,2,0:T(8,128)(2,1)S(1)}, bf16[2,1280,320]{1,2,0:T(8,128)(2,1)}, u32[]{:S(2)}) copy-start(bf16[2,1280,320]{1,2,0:T(8,128)(2,1)} %param.7) | copy-start | bytes 4915204
  7.2 67.4 %all-gather.5.cloned.1.call-start = ((), (), s32[]{:S(2)}) async-start(), calls=%async_computation.7 | async-start | bytes 5570560 | tf_op jit(solution)/shard_map/all_gather | solution.py:38
  33.3 81.8 %all-gather.3.cloned.1.call-start = ((), (), s32[]{:S(2)}) async-start(), calls=%async_computation.6 | async-start | bytes 5570560 | tf_op jit(solution)/shard_map/all_gather | solution.py:39
  48.9 147.8 %reduce-scatter.3.cloned.1.call-start = ((), (), s32[]{:S(2)}) async-start(), calls=%async_computation.8 | async-start | bytes 5570560 | tf_op jit(solution)/shard_map/reduce_scatter | solution.py:57
  121.0 1.1 copy-start.2
  126.7 142.9 %reduce-scatter.5.cloned.1.call-start = ((), (), s32[]{:S(2)}) async-start(), calls=%async_computation.9 | async-start | bytes 5570560 | tf_op jit(solution)/shard_map/reduce_scatter | solution.py:54
  198.7 73.0 %all-to-all-start.2 = ((bf16[64,2,1280]{2,1,0:T(2,128)(2,1)}), bf16[64,2,1280]{2,1,0:T(2,128)(2,1)S(1)}, u32[]{:S(2)}, u32[]{:S(2)}) async-start(bf16[64,2,1280]{2,1,0:T(2,128)(2,1)} %copy.17), calls=%async_computation.3 | async-start | bytes 655360 | tf_op jit(solution)/shard_map/all_to_all | solution.py:65
  271.7 16.5 %all-to-all-start.3 = ((bf16[64,2,1280]{2,1,0:T(2,128)(2,1)}), bf16[64,2,1280]{2,1,0:T(2,128)(2,1)S(1)}, u32[]{:S(2)}, u32[]{:S(2)}) async-start(bf16[64,2,1280]{2,1,0:T(2,128)(2,1)} %copy.19), calls=%async_computation.5 | async-start | bytes 655360 | tf_op jit(solution)/shard_map/all_to_all | solution.py:62
  278.5 161.2 %all-reduce.2.cloned.1.call-start = ((), (), s32[]{:S(2)}) async-start(), calls=%async_computation.10 | async-start | bytes 163840 | tf_op jit(solution)/shard_map/psum | solution.py:82
  295.4 4.1 copy-start.1
Sparse Core Ops, SparseCore 0:
  33.4 41.2 all-gather.4
  76.3 38.7 all-gather.2
  126.9 69.7 reduce-scatter.2
  199.5 70.1 reduce-scatter.4
  305.5 134.0 all-reduce.1
where the time goes:
time: 448 us
  waiting for transfers between devices  308 us (69%)
  matrix products  75.6 us (17%)
  blocking collectives  27.1 us (6%)
  between operations  13.9 us (3%)
  starting transfers between devices  11.8 us (3%)
  local copies, waits for them, and re-layouts  9.08 us (2%)
    psum x1, waiting for transfers between devices, shards(): router_grad = lax.psum(router_term, ('dp', 'expert'))  128 us
    reduce_scatter x1, waiting for transfers between devices, shards(): lax.psum_scatter(part_out.astype(jnp.bfloat16), 'dp', scatter_dimension=0...  60.3 us
    reduce_scatter x1, waiting for transfers between devices, shards(): lax.psum_scatter(part_in.astype(jnp.bfloat16), 'dp', scatter_dimension=0,...  56.5 us
    all_gather x1, waiting for transfers between devices, shards(): lax.all_gather(moved_grad, 'dp', axis=0, tiled=True)  32.9 us
    all_gather x1, waiting for transfers between devices, shards(): lax.all_gather(moved_in, 'dp', axis=0, tiled=True)  25.7 us
    all_to_all x1, blocking collectives, shards(): lax.all_to_all(slot_in, 'expert', split_axis=1, concat_axis=0, tiled=True)  16.4 us
    all_to_all x1, blocking collectives, shards(): lax.all_to_all(slot_grad, 'expert', split_axis=1, concat_axis=0, tiled=True)  10.8 us
  transfers between devices with their start and end apart: 7, of which 6 were waited for; matrix products, arithmetic and copies ran while one was open for 10% of the time, Pallas kernels for 0%

commit v1 on v0

v1 whole, which is shorter than its diff:
```python
import jax
import jax.numpy as jnp
from jax import lax
from jax.experimental import pallas as pl
from jax.experimental.pallas import tpu as pltpu
from jax.sharding import PartitionSpec as P

MESH = pl.DeviceIdType.MESH
BF = jnp.bfloat16
F32 = jnp.float32

D = 1280
M = 256
S = 16
IMG = 8
HID = 320
HID2 = 640
ROWS = 512

root_half = 0.7071067811865476
inv_root_tau = 0.3989422804014327

NT = (((1,), (1,)), ((), ()))
TN = (((0,), (0,)), ((), ()))


def dot(a, b):
    return jnp.dot(a, b, preferred_element_type=F32)


def dot_nt(a, b):
    return lax.dot_general(a, b, NT, preferred_element_type=F32)


def dot_tn(a, b):
    return lax.dot_general(a, b, TN, preferred_element_type=F32)


def permute_rows(source_of, value):
    r = lax.broadcasted_iota(jnp.int32, (128, 128), 0)
    c = lax.broadcasted_iota(jnp.int32, (128, 128), 1)
    matrix = jnp.where(c == source_of(r), 1.0, 0.0).astype(BF)
    return dot(matrix, value).astype(BF)


def by_slot(r):
    return (r & 7) * 16 + (r >> 3)


def by_image(r):
    return (r & 15) * 8 + (r >> 4)


def by_expert(r):
    return ((r >> 3) & 7) * 16 + (r >> 6) * 8 + (r & 7)


def by_peer(r):
    return ((r >> 3) & 1) * 64 + (r >> 4) * 8 + (r & 7)


def rows16(index):
    return pl.ds(pl.multiple_of(index * 16, 16), 16)


def kernel(
    tok_h, grad_h, rt_ref, w1_h, w2_h,
    token_grad_h, router_out, dw1_h, dw2_h,
    tok, grad, w1, w2, disp, comb, stage, a2a_s, a2a_r, rows, parts, rsb,
    hid, act, act_t, dwk, dws, dwr, fin, back_s, back_r, sb, lg, tgo,
    arp, arr, ars, arg, arf,
    s_load, s_w, s_wr, s_a2a, r_a2a, s_ag, r_ag, s_rs, r_rs, s_bk, r_bk,
    s_dw, r_dw, s_out, s_dwo, s_ar1, r_ar1, s_ar2, r_ar2, s_ar3, r_ar3, s_loc,
):
    dp = lax.axis_index("dp")
    ex = lax.axis_index("expert")
    x, zl, core = dp // 4, (dp // 2) % 2, dp % 2
    zh, y = ex // 4, ex % 4

    def in_dp(dx, dz, dc=0):
        return (((x + dx) % 4) * 4 + ((zl + dz) % 2) * 2 + (core + dc) % 2, ex)

    def ex_of(k, sign=1):
        return ((zh + k // 4) % 2) * 4 + (y + 4 + sign * (k % 4)) % 4

    def remote(src, dst, s_sem, r_sem, device):
        return pltpu.make_async_remote_copy(
            src_ref=src, dst_ref=dst, send_sem=s_sem, recv_sem=r_sem,
            device_id=device, device_id_type=MESH,
        )

    barrier = pltpu.get_barrier_semaphore()
    for n in range(1, 16):
        pl.semaphore_signal(
            barrier, inc=1, device_id=in_dp(n // 4, (n // 2) % 2, n % 2), device_id_type=MESH
        )
    for k in range(1, 8):
        pl.semaphore_signal(barrier, inc=1, device_id=(dp, ex_of(k)), device_id_type=MESH)

    def load(which, i):
        src, dst = ((tok_h, tok), (grad_h, grad))[which]
        return pltpu.make_async_copy(src.at[i], dst.at[i], s_load.at[which, i])

    for which in range(2):
        for i in range(IMG):
            load(which, i).start()
    own_w = []
    for j in range(2):
        for n, (src, dst) in enumerate(((w1_h, w1), (w2_h, w2))):
            own_w.append(pltpu.make_async_copy(
                src.at[j], dst.at[j, pl.ds(0, HID)], s_loc.at[n, j]))
    for cp in own_w:
        cp.start()

    rt = rt_ref[...]

    def pre_in(i, carry):
        load(0, i).wait()
        image = tok[i]
        logits = dot_nt(rt, image)
        e1 = jnp.exp(logits - jnp.max(logits, axis=1, keepdims=True))
        d = e1 / jnp.sum(e1, axis=1, keepdims=True)
        e0 = jnp.exp(logits - jnp.max(logits, axis=0, keepdims=True))
        c = e0 / jnp.sum(e0, axis=0, keepdims=True)
        disp[i] = d
        comb[i] = c
        stage[rows16(i)] = dot(d.astype(BF), image).astype(BF)
        return carry

    def pre_grad(i, carry):
        load(1, i).wait()
        stage[rows16(i)] = dot(comb[i].astype(BF), grad[i]).astype(BF)
        return carry

    def start_a2a(a):
        a2a_s[a] = permute_rows(by_slot, stage[...])
        cps = []
        for k in range(1, 8):
            cp = remote(
                a2a_s.at[a, rows16(ex_of(k))], a2a_r.at[a, pl.ds(k * 16, 16)],
                s_a2a.at[a, k], r_a2a.at[a, k], (dp, ex_of(k)),
            )
            cp.start()
            cps.append(cp)
        a2a_r[a, pl.ds(0, 16)] = a2a_s[a, rows16(ex)]
        return cps

    lax.fori_loop(0, IMG, pre_in, 0)
    pl.semaphore_wait(barrier, 22)
    a2a = [start_a2a(0)]
    far_w = []
    for n, (src, dst) in enumerate(((w1_h, w1), (w2_h, w2))):
        for j in range(2):
            cp = remote(
                src.at[j], dst.at[j, pl.ds(HID, HID)], s_w.at[n, j], s_wr.at[n, j], in_dp(0, 0, 1)
            )
            cp.start()
            far_w.append(cp)
    lax.fori_loop(0, IMG, pre_grad, 0)
    a2a.append(start_a2a(1))

    ag = {}

    def ag_copy(a, j, src_slot, dst_slot, dx, dz):
        cp = remote(
            rows.at[a, j, pl.ds(src_slot * 64, 64)], rows.at[a, j, pl.ds(dst_slot * 64, 64)],
            s_ag.at[a, j, dst_slot], r_ag.at[a, j, dst_slot], in_dp(dx, dz),
        )
        cp.start()
        ag[a, j, dst_slot] = cp

    def ag_begin(a):
        for cp in a2a[a]:
            cp.wait_recv()
        ordered = permute_rows(by_expert, a2a_r[a])
        for j in range(2):
            rows[a, j, pl.ds(0, 64)] = ordered[j * 64 : j * 64 + 64]
        ag_copy(a, 0, 0, 1, 0, 1)
        for dx in (1, 3, 2):
            for j in range(2):
                ag_copy(a, j, 0, 2 * dx, dx, 0)
        ag_copy(a, 1, 0, 1, 0, 1)

    def ag_forward(a):
        ag[a, 0, 1].wait_recv()
        for dx in (1, 3, 2):
            ag_copy(a, 0, 1, 2 * dx + 1, dx, 0)
        for dx in (1, 3, 2):
            ag[a, 1, 2 * dx].wait_recv()
            ag_copy(a, 1, 2 * dx, 2 * dx + 1, 0, 1)

    def ag_end(a, j):
        skip = (1,) if j == 0 else (2, 4, 6)
        for slot in range(1, 8):
            if slot not in skip:
                ag[a, j, slot].wait_recv()

    def project(a, w, j, finish):
        for h in range(2):
            hid[j, pl.ds(h * 256, 256)] = finish(
                j, h, dot_nt(rows[a, j, pl.ds(h * 256, 256)], w[j]))

    def keep(j, h, value):
        return value

    def gelu(j):
        def step(n, carry):
            at = pl.ds(pl.multiple_of(n * 32, 32), 32)
            v = hid[j, at]
            half = 0.5 * (1.0 + lax.erf(v * root_half))
            act[j, at] = (v * half).astype(BF)
            hid[j, at] = half + v * jnp.exp(-0.5 * v * v) * inv_root_tau
            return carry

        lax.fori_loop(0, ROWS // 32, step, 0)

    def slope(j, h, value):
        return value * hid[j, pl.ds(h * 256, 256)]

    def to_parts(o, w, j):
        def step(n, carry):
            at = pl.ds(pl.multiple_of(n * 256, 256), 256)
            parts[o, j, :, at] = dot(act[j], w[j, :, at]).astype(BF)
            return carry

        lax.fori_loop(0, D // 256, step, 0)

    dw = []

    def weight_grad(n, a, j):
        def step(m, carry):
            at = pl.ds(pl.multiple_of(m * 256, 256), 256)
            total = dot(act_t[...], rows[a, j, :, at])
            dwk[n, j, :, at] = total[:HID]
            dws[n, j, :, at] = total[HID:].astype(BF)
            return carry

        lax.fori_loop(0, D // 256, step, 0)
        cp = remote(dws.at[n, j], dwr.at[n, j], s_dw.at[n, j], r_dw.at[n, j], in_dp(0, 0, 1))
        cp.start()
        dw.append((cp, n, j))

    rs = {}

    def rs_copy(o, j, slot, land, dx, dz):
        cp = remote(
            parts.at[o, j, pl.ds(slot * 64, 64)], rsb.at[o, j, land],
            s_rs.at[o, j, land], r_rs.at[o, j, land], in_dp(dx, dz),
        )
        cp.start()
        rs[o, j, land] = cp

    def rs_begin(o, j):
        if j == 0:
            for dx in (2, 1, 3):
                for dz in (1, 0):
                    rs_copy(o, j, 2 * dx + dz, 2 * (dx - 1) + dz, 4 - dx, 0)
        else:
            for dx in (2, 1, 3, 0):
                rs_copy(o, j, 2 * dx + 1, dx, 0, 1)

    def part(o, j, slot):
        return parts[o, j, pl.ds(slot * 64, 64)].astype(F32)

    def landed(o, j, land):
        rs[o, j, land].wait_recv()
        return rsb[o, j, land].astype(F32)

    def rs_middle(o, j):
        if j == 0:
            total = part(o, j, 1)
            for dx in (1, 3, 2):
                total = total + landed(o, j, 2 * (dx - 1) + 1)
            parts[o, j, pl.ds(64, 64)] = total.astype(BF)
            rs_copy(o, j, 1, 6, 0, 1)
        else:
            for dx in (2, 1, 3):
                total = part(o, j, 2 * dx) + landed(o, j, dx)
                parts[o, j, pl.ds(128 * dx, 64)] = total.astype(BF)
                rs_copy(o, j, 2 * dx, 3 + dx, 4 - dx, 0)

    def rs_end(o, j):
        total = part(o, j, 0)
        if j == 0:
            lands = (0, 4, 2, 6)
        else:
            lands = (0, 4, 6, 5)
        for land in lands:
            total = total + landed(o, j, land)
        fin[pl.ds(64 * j, 64)] = total.astype(BF)

    def give_back(o):
        back_s[o] = permute_rows(by_peer, fin[...])
        cps = []
        for k in range(1, 8):
            cp = remote(
                back_s.at[o, pl.ds(k * 16, 16)], back_r.at[o, rows16(ex)],
                s_bk.at[o, k], r_bk.at[o, k], (dp, ex_of(k, -1)),
            )
            cp.start()
            cps.append(cp)
        back_r[o, rows16(ex)] = back_s[o, pl.ds(0, 16)]
        return cps

    def take_back(o, cps):
        for cp in cps:
            cp.wait_recv()
        return permute_rows(by_image, back_r[o])

    ag_begin(0)
    ag_begin(1)
    ag_forward(0)
    for cp in own_w:
        cp.wait()
    for cp in far_w:
        cp.wait_recv()
    for j in range(2):
        ag_end(0, j)
        project(0, w1, j, keep)
        if j == 0:
            ag_forward(1)
        gelu(j)
        to_parts(0, w2, j)
        rs_begin(0, j)
    for j in range(2):
        ag_end(1, j)
        act_t[...] = act[j].T
        weight_grad(1, 1, j)
        project(1, w2, j, slope)
        act[j] = hid[j].astype(BF)
        to_parts(1, w1, j)
        rs_begin(1, j)
        if j == 0:
            rs_middle(0, 0)
        act_t[...] = act[j].T
        weight_grad(0, 0, j)
    rs_middle(0, 1)
    rs_end(0, 0)
    rs_end(0, 1)
    backs = [give_back(0)]
    rs_middle(1, 0)
    rs_middle(1, 1)

    for cp, n, j in dw:
        cp.wait()
        dws[n, j] = (dwk[n, j] + dwr[n, j].astype(F32)).astype(BF)
        out = (dw1_h, dw2_h)[n]
        pltpu.make_async_copy(dws.at[n, j], out.at[j], s_dwo.at[n, j]).start()

    sb[0] = take_back(0, backs[0])

    def comb_side(i, carry):
        g = dot_nt(sb[0, rows16(i)], grad[i])
        c = comb[i]
        comb[i] = c * (g - jnp.sum(c * g, axis=0, keepdims=True))
        return carry

    lax.fori_loop(0, IMG, comb_side, 0)

    rs_end(1, 0)
    rs_end(1, 1)
    backs.append(give_back(1))
    sb[1] = take_back(1, backs[1])

    def disp_side(i, total):
        g = dot_nt(sb[1, rows16(i)], tok[i])
        d = disp[i]
        grad_logit = (comb[i] + d * (g - jnp.sum(d * g, axis=1, keepdims=True))).astype(BF)
        lg[i] = grad_logit
        return total + dot(grad_logit, tok[i])

    term = lax.fori_loop(0, IMG, disp_side, jnp.zeros((S, D), F32))
    for p in range(8):
        lane = 384 * (p // 2)
        width = min(384, D - lane)
        arp[p, :, pl.ds(0, width)] = term[8 * (p % 2) : 8 * (p % 2) + 8, lane : lane + width]
        if width < 384:
            arp[p, :, pl.ds(width, 384 - width)] = jnp.zeros((8, 384 - width), F32)

    ar1 = []
    for k in range(1, 8):
        cp = remote(arp.at[ex_of(k)], arr.at[k], s_ar1.at[k], r_ar1.at[k], (dp, ex_of(k)))
        cp.start()
        ar1.append(cp)

    def out_copy(i):
        return pltpu.make_async_copy(tgo.at[i % 2], token_grad_h.at[i], s_out.at[i])

    def token_side(first, last):
        for i in range(first, last):
            if i >= 2:
                out_copy(i - 2).wait()
            left = jnp.concatenate([disp[i].astype(BF), lg[i]], axis=0)
            right = jnp.concatenate([sb[1, pl.ds(i * 16, 16)], rt], axis=0)
            tgo[i % 2] = dot_tn(left, right).astype(BF)
            out_copy(i).start()

    token_side(0, 3)
    total = arp[ex]
    for k, cp in enumerate(ar1, 1):
        cp.wait_recv()
        total = total + arr[k]
    ars[...] = total
    ar2 = []
    for n in range(1, 16):
        cp = remote(
            ars, arg.at[dp], s_ar2.at[n], r_ar2.at[n], in_dp(n // 4, (n // 2) % 2, n % 2))
        cp.start()
        ar2.append(cp)
    arg[dp] = total
    token_side(3, 6)
    for cp in ar2:
        cp.wait_recv()
    total = arg[0]
    for n in range(1, 16):
        total = total + arg[n]
    for cp in ar2:
        cp.wait_send()
    ars[...] = total
    ar3 = []
    for k in range(1, 8):
        cp = remote(ars, arf.at[ex], s_ar3.at[k], r_ar3.at[k], (dp, ex_of(k)))
        cp.start()
        ar3.append(cp)
    arf[ex] = total
    token_side(6, 8)
    for cp in ar3:
        cp.wait()
    for p in range(8):
        lane = 384 * (p // 2)
        width = min(384, D - lane)
        router_out[pl.ds(8 * (p % 2), 8), pl.ds(lane, width)] = arf[p, :, pl.ds(0, width)]

    out_copy(6).wait()
    out_copy(7).wait()
    for n in range(2):
        for j in range(2):
            out = (dw1_h, dw2_h)[n]
            pltpu.make_async_copy(dws.at[n, j], out.at[j], s_dwo.at[n, j]).wait()
    for group in (a2a[0], a2a[1], far_w, ag.values(), rs.values(), backs[0], backs[1], ar1):
        for cp in group:
            cp.wait_send()


def shards(tokens, router, weight_in, weight_out, out_grad):
    any_space = pl.BlockSpec(memory_space=pl.ANY)
    vmem = pl.BlockSpec(memory_space=pltpu.VMEM)
    dma = pltpu.SemaphoreType.DMA
    V = pltpu.VMEM
    token_grad, router_grad, dw1, dw2 = pl.pallas_call(
        kernel,
        name="soft_moe",
        out_shape=(
            jax.ShapeDtypeStruct((IMG, M, D), BF),
            jax.ShapeDtypeStruct((S, D), F32),
            jax.ShapeDtypeStruct((2, HID, D), BF),
            jax.ShapeDtypeStruct((2, HID, D), BF),
        ),
        in_specs=[any_space, any_space, vmem, any_space, any_space],
        out_specs=(any_space, vmem, any_space, any_space),
        scratch_shapes=[
            V((IMG, M, D), BF), V((IMG, M, D), BF),
            V((2, HID2, D), BF), V((2, HID2, D), BF),
            V((IMG, S, M), F32), V((IMG, S, M), F32),
            V((128, D), BF), V((2, 128, D), BF), V((2, 128, D), BF),
            V((2, 2, ROWS, D), BF), V((2, 2, ROWS, D), BF),
            V((2, 2, 7, 64, D), BF),
            V((2, ROWS, HID2), F32), V((2, ROWS, HID2), BF), V((HID2, ROWS), BF),
            V((2, 2, HID, D), F32), V((2, 2, HID, D), BF), V((2, 2, HID, D), BF),
            V((128, D), BF), V((2, 128, D), BF), V((2, 128, D), BF),
            V((2, 128, D), BF), V((IMG, S, M), BF), V((2, M, D), BF),
            V((8, 8, 384), F32), V((8, 8, 384), F32), V((8, 384), F32),
            V((16, 8, 384), F32), V((8, 8, 384), F32),
            dma((2, IMG)), dma((2, 2)), dma((2, 2)), dma((2, 8)), dma((2, 8)),
            dma((2, 2, 8)), dma((2, 2, 8)), dma((2, 2, 7)), dma((2, 2, 7)),
            dma((2, 8)), dma((2, 8)), dma((2, 2)), dma((2, 2)), dma((IMG,)), dma((2, 2)),
            dma((8,)), dma((8,)), dma((16,)), dma((16,)), dma((8,)), dma((8,)), dma((2, 2)),
        ],
        compiler_params=pltpu.CompilerParams(
            collective_id=0, has_side_effects=True, vmem_limit_bytes=62 * 2**20
        ),
    )(tokens, out_grad, router.T, jnp.swapaxes(weight_in, 1, 2), weight_out)
    return token_grad, router_grad.T, jnp.swapaxes(dw1, 1, 2), dw2


def solution(mesh):
    in_specs = (
        P(("dp", "expert"), None, None),
        P(),
        P("expert", None, "dp"),
        P("expert", "dp", None),
        P(("dp", "expert"), None, None),
    )
    out_specs = (
        P(("dp", "expert"), None, None),
        P(),
        P("expert", None, "dp"),
        P("expert", "dp", None),
    )
    return jax.shard_map(shards, mesh=mesh, in_specs=in_specs, out_specs=out_specs, check_vma=False)
```

time: 448 us -> 156 us (0.35)
  waiting for transfers between devices: 308 us -> 0 us
  Pallas kernels: 0 us -> 146 us
  matrix products: 75.6 us -> 0 us
  blocking collectives: 27.1 us -> 0 us
  between operations: 13.9 us -> 0.66 us
  starting transfers between devices: 11.8 us -> 0 us
    pallas_call x0 -> x1, Pallas kernels: none -> 146 us  [shards(): pl.pallas_call(kernel, name='soft_moe', out_shape=(jax.ShapeDtypeStruct((...]
    psum x1 -> x0, waiting for transfers between devices: 128 us -> none  [shards(): router_grad = lax.psum(router_term, ('dp', 'expert'))]
    reduce_scatter x2 -> x0, waiting for transfers between devices: 117 us -> none  [the longest x1 60.3 us: shards(): lax.psum_scatter(part_out.astype(jnp.bfloat16), 'dp', scatter_dimension=0...]
    dot_general x13 -> x0, matrix products: 68.7 us -> none  [the longest x1 7.53 us: shards(): jnp.einsum('rjd,jdf->rjf', rows_in, weight_in, preferred_element_type=jnp...]
    all_gather x2 -> x0, waiting for transfers between devices: 58.6 us -> none  [the longest x1 32.9 us: shards(): lax.all_gather(moved_grad, 'dp', axis=0, tiled=True)]
    all_to_all x2 -> x0, blocking collectives: 27.1 us -> none  [the longest x1 16.4 us: shards(): lax.all_to_all(slot_in, 'expert', split_axis=1, concat_axis=0, tiled=True)]
    all_to_all x2 -> x0, starting transfers between devices: 11.6 us -> none  [the longest x1 6.85 us: shards(): lax.all_to_all(summed_out.astype(jnp.bfloat16), 'expert', split_axis=0, c...]
    sub x1 -> x0, matrix products: 6.86 us -> none  [shards(): grad_comb - jnp.sum(combine * grad_comb, axis=1, keepdims=True)]
  transfers between devices with their start and end apart: 7 -> 0, of which waited for: 6 -> 0; matrix products, arithmetic and copies ran while one was open for 10% -> 0% of each run, Pallas kernels for 0% -> 0%
where the time goes in v1:
time: 156 us
  Pallas kernels  146 us (94%)
  local copies, waits for them, and re-layouts  9.15 us (6%)
    pallas_call x1, Pallas kernels, shards(): pl.pallas_call(kernel, name='soft_moe', out_shape=(jax.ShapeDtypeStruct((...  146 us
    unnamed x10, local copies, waits for them, and re-layouts  9.15 us

profile of v1, /device:TPU:1, one launch (start us, length us, event | category | flops | bytes accessed | tf_op | source)
XLA Modules:
  0.0 156.3 jit_solution(1193114181937304570)
XLA Ops:
  0.6 146.5 %soft_moe.1 = (bf16[8,256,1280]{2,1,0:T(8,128)(2,1)}, f32[16,1280]{1,0:T(8,128)}, bf16[2,320,1280]{2,1,0:T(8,128)(2,1)}, bf16[2,320,1280]{2,1,0:T(8,128)(2,1)}) custom-call(bf16[8,256,1280]{2,1,0:T(8,128)(2,1)} %tok_h.1, bf16[8,256,1280]{2,1,0:T(8,128)(2,1)} %grad_h.1, bf16[16,1280]{1,0:T(8,128)(2,1)} %bitcast.7, bf16[2,320,1280]{2,1,0:T(8,128)(2,1)} %bitcast.4, ...), custom_call_target="tpu_custom_call" | custom-call | tf_op jit(solution)/shard_map/soft_moe/pallas_call | solution.py:450
  147.1 0.0 copy-start.2
  147.1 0.0 copy-start.1
  147.1 5.3 %copy.13 = bf16[8,256,1280]{2,1,0:T(8,128)(2,1)} copy(bf16[8,256,1280]{2,1,0:T(8,128)(2,1)} %get-tuple-element.16) | data formatting | bytes 10485760
  152.5 0.0 copy-done.2
  152.5 0.6 copy.14
  153.1 0.0 copy-done.1
  153.1 0.0 copy-start
  153.1 1.2 copy.15
  154.3 0.9 copy-done
  155.1 1.2 copy.16
Async XLA Ops:
  147.1 5.3 %copy-start.2 = (f32[16,1280]{1,0:T(8,128)S(1)}, f32[16,1280]{1,0:T(8,128)}, u32[]{:S(2)}) copy-start(f32[16,1280]{1,0:T(8,128)} %get-tuple-element.9) | copy-start | bytes 245764
  147.1 6.0 %copy-start.1 = (bf16[2,320,1280]{2,1,0:T(8,128)(2,1)S(1)}, bf16[2,320,1280]{2,1,0:T(8,128)(2,1)}, u32[]{:S(2)}) copy-start(bf16[2,320,1280]{2,1,0:T(8,128)(2,1)} %get-tuple-element.10) | copy-start | bytes 4915204
  153.1 2.0 %copy-start = (bf16[2,320,1280]{2,1,0:T(8,128)(2,1)S(1)}, bf16[2,320,1280]{2,1,0:T(8,128)(2,1)}, u32[]{:S(2)}) copy-start(bf16[2,320,1280]{2,1,0:T(8,128)(2,1)} %get-tuple-element.19) | copy-start | bytes 4915204

commit v2 on v1

v2 whole, which is shorter than its diff:
```python
import jax
import jax.numpy as jnp
from jax import lax
from jax.experimental import pallas as pl
from jax.experimental.pallas import tpu as pltpu
from jax.sharding import PartitionSpec as P

MESH = pl.DeviceIdType.MESH
BF = jnp.bfloat16
F32 = jnp.float32

D = 1280
M = 256
S = 16
IMG = 8
HID = 320
HID2 = 640
ROWS = 512

root_half = 0.7071067811865476
inv_root_tau = 0.3989422804014327

NT = (((1,), (1,)), ((), ()))
TN = (((0,), (0,)), ((), ()))


def dot(a, b):
    return jnp.dot(a, b, preferred_element_type=F32)


def dot_nt(a, b):
    return lax.dot_general(a, b, NT, preferred_element_type=F32)


def dot_tn(a, b):
    return lax.dot_general(a, b, TN, preferred_element_type=F32)


def permute_rows(source_of, value):
    r = lax.broadcasted_iota(jnp.int32, (128, 128), 0)
    c = lax.broadcasted_iota(jnp.int32, (128, 128), 1)
    matrix = jnp.where(c == source_of(r), 1.0, 0.0).astype(BF)
    return dot(matrix, value).astype(BF)


def by_slot(r):
    return (r & 7) * 16 + (r >> 3)


def by_image(r):
    return (r & 15) * 8 + (r >> 4)


def by_expert(r):
    return ((r >> 3) & 7) * 16 + (r >> 6) * 8 + (r & 7)


def by_peer(r):
    return ((r >> 3) & 1) * 64 + (r >> 4) * 8 + (r & 7)


X_FIRST = ((0, 1), (1, 0), (1, 1))


def rows16(index):
    return pl.ds(pl.multiple_of(index * 16, 16), 16)


def kernel(
    tok_h, grad_h, rt_ref, w1_h, w2_h,
    router_out, back_out, disp_out, lg, dw1_h, dw2_h,
    tok, grad, w1, w2, disp, comb, stage, a2a_s, a2a_r, rows, parts, rsb,
    hid, act, act_t, dwk, dws, dwr, fin, back_s, back_r, sb,
    arp, arr, ars, arg, arf,
    s_load, s_w, s_wr, s_a2a, r_a2a, s_ag, r_ag, s_rs, r_rs, s_bk, r_bk,
    s_dw, r_dw, s_dwo, s_ar, r_ar, s_loc,
):
    dp = lax.axis_index("dp")
    ex = lax.axis_index("expert")
    x, zl, core = dp // 4, (dp // 2) % 2, dp % 2
    zh, y = ex // 4, ex % 4

    side = 1 - 2 * core

    def in_dp(dx, dz, dc=0):
        return (((x + 4 + side * dx) % 4) * 4 + ((zl + dz) % 2) * 2 + (core + dc) % 2, ex)

    def ex_of(k, sign=1):
        return ((zh + k // 4) % 2) * 4 + (y + 4 + sign * (k % 4)) % 4

    def peer(k, sign=1):
        flip = (zl + k // 4) % 2
        return (x * 4 + flip * 2 + core, ex_of(k, sign))

    def remote(src, dst, s_sem, r_sem, device):
        return pltpu.make_async_remote_copy(
            src_ref=src, dst_ref=dst, send_sem=s_sem, recv_sem=r_sem,
            device_id=device, device_id_type=MESH,
        )

    barrier = pltpu.get_barrier_semaphore()
    for n in range(1, 16):
        pl.semaphore_signal(
            barrier, inc=1, device_id=in_dp(n // 4, (n // 2) % 2, n % 2), device_id_type=MESH
        )
    for k in range(1, 8):
        pl.semaphore_signal(barrier, inc=1, device_id=peer(k), device_id_type=MESH)

    def load(which, i):
        src, dst = ((tok_h, tok), (grad_h, grad))[which]
        return pltpu.make_async_copy(src.at[i], dst.at[i], s_load.at[which, i])

    for i in range(IMG):
        load(0, i).start()

    rt = rt_ref[...]

    def pre_in(n, carry):
        for u in range(4):
            load(0, 4 * n + u).wait()
            load(1, 4 * n + u).start()
        for u in range(4):
            i = 4 * n + u
            image = tok[i]
            logits = dot_nt(rt, image)
            e1 = jnp.exp(logits - jnp.max(logits, axis=1, keepdims=True))
            d = e1 / jnp.sum(e1, axis=1, keepdims=True)
            e0 = jnp.exp(logits - jnp.max(logits, axis=0, keepdims=True))
            c = e0 / jnp.sum(e0, axis=0, keepdims=True)
            disp[i] = d
            comb[i] = c
            stage[rows16(i)] = dot(d.astype(BF), image).astype(BF)
        return carry

    def pre_grad(n, carry):
        for u in range(4):
            load(1, 4 * n + u).wait()
        for u in range(4):
            i = 4 * n + u
            stage[rows16(i)] = dot(comb[i].astype(BF), grad[i]).astype(BF)
        return carry

    def wait_sent(ref, sem):
        remote(ref, ref, sem, sem, in_dp(1, 0)).wait_send()

    def wait_landed(ref, sem):
        remote(ref, ref, sem, sem, in_dp(1, 0)).wait_recv()

    def start_a2a(a):
        a2a_s[a] = permute_rows(by_slot, stage[...])
        for k in range(1, 8):
            remote(
                a2a_s.at[a, rows16(ex_of(k))], a2a_r.at[a, pl.ds(k * 16, 16)],
                s_a2a.at[a], r_a2a.at[a], peer(k),
            ).start()
        a2a_r[a, pl.ds(0, 16)] = a2a_s[a, rows16(ex)]

    lax.fori_loop(0, IMG // 4, pre_in, 0)
    pl.semaphore_wait(barrier, 22)
    start_a2a(0)
    lax.fori_loop(0, IMG // 4, pre_grad, 0)
    start_a2a(1)

    LAST = ((4, 5, 6, 7), (1, 3, 5, 7))

    def ag_copy(a, j, src_slot, dst_slot, dx, dz):
        sem = 0 if dst_slot in LAST[j] else dst_slot
        remote(
            rows.at[a, j, pl.ds(src_slot * 64, 64)], rows.at[a, j, pl.ds(dst_slot * 64, 64)],
            s_ag.at[a, j], r_ag.at[a, j, sem], in_dp(dx, dz),
        ).start()

    def ag_wait(a, j, slot):
        wait_landed(rows.at[a, j, pl.ds(slot * 64, 64)], r_ag.at[a, j, slot])

    def ag_own(a):
        wait_landed(a2a_r.at[a, pl.ds(16, 112)], r_a2a.at[a])
        ordered = permute_rows(by_expert, a2a_r[a])
        for j in range(2):
            rows[a, j, pl.ds(0, 64)] = ordered[j * 64 : j * 64 + 64]

    def ag_first(a):
        for j in range(2):
            ag_copy(a, j, 0, 2, 1, 0)
            ag_copy(a, j, 0, 1, 0, 1)
            ag_copy(a, j, 0, 6, 3, 0)

    def ag_second(a):
        ag_wait(a, 0, 1)
        ag_copy(a, 0, 1, 3, 1, 0)
        ag_copy(a, 0, 1, 7, 3, 0)
        for j in range(2):
            ag_wait(a, j, 2)
            ag_copy(a, j, 2, 4, 1, 0)
        ag_copy(a, 1, 2, 3, 0, 1)
        ag_wait(a, 1, 6)
        ag_copy(a, 1, 6, 7, 0, 1)

    def ag_third(a):
        ag_wait(a, 0, 3)
        ag_copy(a, 0, 3, 5, 1, 0)
        ag_wait(a, 1, 4)
        ag_copy(a, 1, 4, 5, 0, 1)

    def ag_end(a, j):
        wait_landed(rows.at[a, j, pl.ds(256, 256)], r_ag.at[a, j, 0])

    def project(a, w, j, finish):
        for h in range(2):
            hid[j, pl.ds(h * 256, 256)] = finish(
                j, h, dot_nt(rows[a, j, pl.ds(h * 256, 256)], w[j]))

    def keep(j, h, value):
        return value

    def gelu(j):
        def step(n, carry):
            at = pl.ds(pl.multiple_of(n * 32, 32), 32)
            v = hid[j, at]
            half = 0.5 * (1.0 + lax.erf(v * root_half))
            act[j, at] = (v * half).astype(BF)
            hid[j, at] = half + v * jnp.exp(-0.5 * v * v) * inv_root_tau
            return carry

        lax.fori_loop(0, ROWS // 32, step, 0)

    def slope(j, h, value):
        return value * hid[j, pl.ds(h * 256, 256)]

    def to_parts(o, w, j):
        def step(n, carry):
            at = pl.ds(pl.multiple_of(n * 256, 256), 256)
            parts[o, j, :, at] = dot(act[j], w[j, :, at]).astype(BF)
            return carry

        lax.fori_loop(0, D // 256, step, 0)

    dw = []

    def weight_grad(n, a, j):
        def step(m, carry):
            at = pl.ds(pl.multiple_of(m * 256, 256), 256)
            total = dot(act_t[j], rows[a, j, :, at])
            dwk[n, j, :, at] = total[:HID]
            dws[n, j, :, at] = total[HID:].astype(BF)
            return carry

        lax.fori_loop(0, D // 256, step, 0)
        cp = remote(dws.at[n, j], dwr.at[n, j], s_dw.at[n, j], r_dw.at[n, j], in_dp(0, 0, 1))
        cp.start()
        dw.append((cp, n, j))

    def rs_copy(o, j, first, count, land, sem, dx, dz):
        remote(
            parts.at[o, j, pl.ds(first, count)], rsb.at[o, j, pl.ds(land, count)],
            s_rs.at[o, j], r_rs.at[o, j, sem], in_dp(dx, dz),
        ).start()

    def part(o, j, first, count):
        return parts[o, j, pl.ds(first, count)].astype(F32)

    def landed(o, j, land, count, sem):
        wait_landed(rsb.at[o, j, pl.ds(land, count)], r_rs.at[o, j, sem])
        return rsb[o, j, pl.ds(land, count)].astype(F32)

    def rs_begin(o, j):
        if (o, j) in X_FIRST:
            rs_copy(o, j, 256, 128, 0, 0, 3, 0)
            rs_copy(o, j, 384, 128, 128, 1, 1, 0)
        else:
            for dx in (2, 1, 3, 0):
                rs_copy(o, j, 128 * dx + 64, 64, 64 * dx, 3 + dx, 0, 1)

    def rs_add(o, j, dx):
        total = part(o, j, 128 * dx, 64) + landed(o, j, 64 * dx, 64, 3 + dx)
        parts[o, j, pl.ds(128 * dx, 64)] = total.astype(BF)

    def rs_far(o, j):
        rs_add(o, j, 2)
        rs_copy(o, j, 256, 64, 256, 0, 3, 0)

    def rs_near(o, j):
        rs_add(o, j, 3)
        rs_copy(o, j, 384, 64, 320, 1, 1, 0)
        rs_add(o, j, 1)

    def rs_second(o, j):
        if (o, j) in X_FIRST:
            count, land, last = 128, 0, 256
        else:
            count, land, last = 64, 256, 384
        total = part(o, j, 128, count) + landed(o, j, land, count, 0)
        parts[o, j, pl.ds(128, count)] = total.astype(BF)
        rs_copy(o, j, 128, count, last, 1, 3, 0)

    def rs_third(o, j):
        both = landed(o, j, 128, 256, 1)
        total = part(o, j, 64, 64) + both[64:128] + both[192:256]
        parts[o, j, pl.ds(64, 64)] = total.astype(BF)
        rs_copy(o, j, 64, 64, 384, 2, 0, 1)
        fin[pl.ds(64 * j, 64)] = (part(o, j, 0, 64) + both[:64] + both[128:192])

    def rs_end(o, j):
        if (o, j) in X_FIRST:
            total = fin[pl.ds(64 * j, 64)] + landed(o, j, 384, 64, 2)
        else:
            both = landed(o, j, 320, 128, 1)
            total = part(o, j, 0, 64) + both[:64] + both[64:] + landed(o, j, 0, 64, 3)
        back_s[o, pl.ds(64 * j, 64)] = total.astype(BF)

    def give_back(o):
        back_s[o] = permute_rows(by_peer, back_s[o])
        for k in range(1, 8):
            remote(
                back_s.at[o, pl.ds(k * 16, 16)], back_r.at[o, rows16(ex)],
                s_bk.at[o], r_bk.at[o], peer(k, -1),
            ).start()
        back_r[o, rows16(ex)] = back_s[o, pl.ds(0, 16)]

    def take_back(o):
        wait_landed(back_r.at[o, pl.ds(0, 112)], r_bk.at[o])
        return permute_rows(by_image, back_r[o])

    def hidden_step(j):
        ag_end(0, j)
        project(0, w1, j, keep)
        gelu(j)

    def grad_step(j):
        ag_end(1, j)
        project(1, w2, j, slope)
        act_t[j] = act[j].T
        act[j] = hid[j].astype(BF)
        to_parts(1, w1, j)
        rs_begin(1, j)

    ag_own(0)
    ag_first(0)
    own_w, far_w = [], []
    for n, (src, dst) in enumerate(((w1_h, w1), (w2_h, w2))):
        for j in range(2):
            own_w.append(pltpu.make_async_copy(
                src.at[j], dst.at[j, pl.ds(0, HID)], s_loc.at[n, j]))
            far_w.append(remote(
                src.at[j], dst.at[j, pl.ds(HID, HID)], s_w.at[n, j], s_wr.at[n, j],
                in_dp(0, 0, 1)))
    for cp in own_w + far_w:
        cp.start()
    ag_own(1)
    ag_second(0)
    ag_first(1)
    ag_third(0)
    for cp in own_w:
        cp.wait()
    for cp in far_w:
        cp.wait_recv()
    hidden_step(0)
    ag_second(1)
    to_parts(0, w2, 0)
    rs_begin(0, 0)
    hidden_step(1)
    ag_third(1)
    to_parts(0, w2, 1)
    rs_begin(0, 1)
    grad_step(0)
    rs_second(0, 1)
    grad_step(1)
    rs_far(0, 0)
    rs_near(0, 0)
    weight_grad(1, 1, 0)
    rs_third(0, 1)
    rs_second(1, 0)
    rs_second(0, 0)
    weight_grad(1, 1, 1)
    rs_second(1, 1)
    rs_third(1, 0)
    rs_end(0, 0)
    rs_end(0, 1)
    give_back(0)
    act_t[0] = act[0].T
    weight_grad(0, 0, 0)
    rs_third(1, 1)
    act_t[1] = act[1].T
    weight_grad(0, 0, 1)
    sb[0] = take_back(0)

    def comb_side(n, carry):
        for u in range(4):
            i = 4 * n + u
            g = dot_nt(sb[0, rows16(i)], grad[i])
            c = comb[i]
            comb[i] = c * (g - jnp.sum(c * g, axis=0, keepdims=True))
        return carry

    lax.fori_loop(0, IMG // 4, comb_side, 0)

    rs_end(1, 0)
    rs_end(1, 1)
    give_back(1)

    for cp, n, j in dw:
        cp.wait()
        dws[n, j] = (dwk[n, j] + dwr[n, j].astype(F32)).astype(BF)
        out = (dw1_h, dw2_h)[n]
        pltpu.make_async_copy(dws.at[n, j], out.at[j], s_dwo.at[n, j]).start()

    sb[1] = take_back(1)
    back_out[...] = sb[1]
    for i in range(IMG):
        disp_out[i] = disp[i].astype(BF)

    def disp_side(n, total):
        for u in range(4):
            i = 4 * n + u
            g = dot_nt(sb[1, rows16(i)], tok[i])
            d = disp[i]
            lg[i] = (comb[i] + d * (g - jnp.sum(d * g, axis=1, keepdims=True))).astype(BF)
        for u in range(4):
            i = 4 * n + u
            total = total + dot(lg[i], tok[i])
        return total

    term = lax.fori_loop(0, IMG // 4, disp_side, jnp.zeros((S, D), F32))
    for p in range(8):
        lane = 384 * (p // 2)
        width = min(384, D - lane)
        arp[p, :, pl.ds(0, width)] = term[8 * (p % 2) : 8 * (p % 2) + 8, lane : lane + width]
        if width < 384:
            arp[p, :, pl.ds(width, 384 - width)] = jnp.zeros((8, 384 - width), F32)

    for k in range(1, 8):
        remote(arp.at[ex_of(k)], arr.at[k], s_ar.at[0], r_ar.at[0], peer(k)).start()
    for n in range(2):
        wait_sent(a2a_s.at[n, pl.ds(0, 112)], s_a2a.at[n])
        wait_sent(back_s.at[n, pl.ds(0, 112)], s_bk.at[n])
        for j in range(2):
            wait_sent(rows.at[n, j, pl.ds(64, 448)], s_ag.at[n, j])
            wait_sent(rsb.at[n, j], s_rs.at[n, j])
    wait_landed(arr.at[pl.ds(1, 7)], r_ar.at[0])
    total = arp[ex]
    for k in range(1, 8):
        total = total + arr[k]
    ars[0] = total
    for n in range(1, 16):
        remote(
            ars.at[0], arg.at[dp], s_ar.at[1], r_ar.at[1], in_dp(n // 4, (n // 2) % 2, n % 2)
        ).start()
    arg[dp] = total
    for cp in far_w:
        cp.wait_send()
    for n in range(2):
        for j in range(2):
            out = (dw1_h, dw2_h)[n]
            pltpu.make_async_copy(dws.at[n, j], out.at[j], s_dwo.at[n, j]).wait()
    wait_landed(arg.at[pl.ds(0, 15)], r_ar.at[1])
    total = arg[0]
    for n in range(1, 16):
        total = total + arg[n]
    ars[1] = total
    for k in range(1, 8):
        remote(ars.at[1], arf.at[ex], s_ar.at[2], r_ar.at[2], peer(k)).start()
    arf[ex] = total
    wait_sent(arp.at[pl.ds(0, 7)], s_ar.at[0])
    wait_sent(arg.at[pl.ds(0, 15)], s_ar.at[1])
    wait_landed(arf.at[pl.ds(0, 7)], r_ar.at[2])
    for p in range(8):
        lane = 384 * (p // 2)
        width = min(384, D - lane)
        router_out[pl.ds(8 * (p % 2), 8), pl.ds(lane, width)] = arf[p, :, pl.ds(0, width)]
    wait_sent(arf.at[pl.ds(0, 7)], s_ar.at[2])


def token_kernel(
    rt_ref, router_ref, back_ref, disp_ref, lg_ref, dw1_in, dw2_in,
    token_grad_h, router_out, dw1_h, dw2_h, tgo, dwv, s_out, s_in, s_dw,
):
    reads, writes = [], []
    for n, (src, dst) in enumerate(((dw1_in, dw1_h), (dw2_in, dw2_h))):
        reads.append(pltpu.make_async_copy(src, dwv.at[n], s_in.at[n]))
        writes.append(pltpu.make_async_copy(dwv.at[n], dst, s_dw.at[n]))
    for cp in reads:
        cp.start()
    router_out[...] = router_ref[...]
    for i in range(IMG):
        left = jnp.concatenate([disp_ref[i], lg_ref[i]], axis=0)
        right = jnp.concatenate([back_ref[pl.ds(i * 16, 16)], rt_ref[...]], axis=0)
        tgo[i] = dot_tn(left, right).astype(BF)
        cp = pltpu.make_async_copy(tgo.at[i], token_grad_h.at[i], s_out.at[i])
        cp.start()
        writes.append(cp)
        if i in (2, 4):
            reads[i // 2 - 1].wait()
            writes[i // 2 - 1].start()
    for cp in writes:
        cp.wait()


def shards(tokens, router, weight_in, weight_out, out_grad):
    any_space = pl.BlockSpec(memory_space=pl.ANY)
    vmem = pl.BlockSpec(memory_space=pltpu.VMEM)
    dma = pltpu.SemaphoreType.DMA
    V = pltpu.VMEM
    router_t = router.T
    router_grad, back, disp_half, grad_logit, dw1, dw2 = pl.pallas_call(
        kernel,
        name="soft_moe",
        out_shape=(
            jax.ShapeDtypeStruct((S, D), F32),
            jax.ShapeDtypeStruct((128, D), BF),
            jax.ShapeDtypeStruct((IMG, S, M), BF),
            jax.ShapeDtypeStruct((IMG, S, M), BF),
            jax.ShapeDtypeStruct((2, HID, D), BF),
            jax.ShapeDtypeStruct((2, HID, D), BF),
        ),
        in_specs=[any_space, any_space, vmem, any_space, any_space],
        out_specs=(vmem, vmem, vmem, vmem, any_space, any_space),
        scratch_shapes=[
            V((IMG, M, D), BF), V((IMG, M, D), BF),
            V((2, HID2, D), BF), V((2, HID2, D), BF),
            V((IMG, S, M), F32), V((IMG, S, M), F32),
            V((128, D), BF), V((2, 128, D), BF), V((2, 128, D), BF),
            V((2, 2, ROWS, D), BF), V((2, 2, ROWS, D), BF),
            V((2, 2, 448, D), BF),
            V((2, ROWS, HID2), F32), V((2, ROWS, HID2), BF), V((2, HID2, ROWS), BF),
            V((2, 2, HID, D), F32), V((2, 2, HID, D), BF), V((2, 2, HID, D), BF),
            V((128, D), F32), V((2, 128, D), BF), V((2, 128, D), BF),
            V((2, 128, D), BF),
            V((8, 8, 384), F32), V((8, 8, 384), F32), V((2, 8, 384), F32),
            V((16, 8, 384), F32), V((8, 8, 384), F32),
            dma((2, IMG)), dma((2, 2)), dma((2, 2)), dma((2,)), dma((2,)),
            dma((2, 2)), dma((2, 2, 8)), dma((2, 2)), dma((2, 2, 8)),
            dma((2,)), dma((2,)), dma((2, 2)), dma((2, 2)), dma((2, 2)),
            dma((3,)), dma((3,)), dma((2, 2)),
        ],
        compiler_params=pltpu.CompilerParams(
            collective_id=0, has_side_effects=True, vmem_limit_bytes=62 * 2**20
        ),
    )(tokens, out_grad, router_t, jnp.swapaxes(weight_in, 1, 2), weight_out)
    token_grad, router_grad, dw1, dw2 = pl.pallas_call(
        token_kernel,
        name="token_grad",
        out_shape=(
            jax.ShapeDtypeStruct((IMG, M, D), BF),
            jax.ShapeDtypeStruct((S, D), F32),
            jax.ShapeDtypeStruct((2, HID, D), BF),
            jax.ShapeDtypeStruct((2, HID, D), BF),
        ),
        in_specs=[vmem] * 5 + [any_space] * 2,
        out_specs=(any_space, vmem, any_space, any_space),
        scratch_shapes=[
            V((IMG, M, D), BF), V((2, 2, HID, D), BF), dma((IMG,)), dma((2,)), dma((2,)),
        ],
        compiler_params=pltpu.CompilerParams(vmem_limit_bytes=62 * 2**20),
    )(router_t, router_grad, back, disp_half, grad_logit, dw1, dw2)
    return token_grad, router_grad.T, jnp.swapaxes(dw1, 1, 2), dw2


def solution(mesh):
    in_specs = (
        P(("dp", "expert"), None, None),
        P(),
        P("expert", None, "dp"),
        P("expert", "dp", None),
        P(("dp", "expert"), None, None),
    )
    out_specs = (
        P(("dp", "expert"), None, None),
        P(),
        P("expert", None, "dp"),
        P("expert", "dp", None),
    )
    return jax.shard_map(shards, mesh=mesh, in_specs=in_specs, out_specs=out_specs, check_vma=False)
```

time: 156 us -> 136 us (0.87)
  Pallas kernels: 146 us -> 135 us
  local copies, waits for them, and re-layouts: 9.15 us -> 0 us
    pallas_call x1, Pallas kernels: 146 us -> 129 us  [shards(): pl.pallas_call(kernel, name='soft_moe', out_shape=(jax.ShapeDtypeStruct((...]
    unnamed x10 -> x0, local copies, waits for them, and re-layouts: 9.15 us -> none
    pallas_call x0 -> x1, Pallas kernels: none -> 6.28 us  [shards(): pl.pallas_call(token_kernel, name='token_grad', out_shape=(jax.ShapeDtype...]
where the time goes in v2:
time: 136 us
  Pallas kernels  135 us (99%)
    pallas_call x1, Pallas kernels, shards(): pl.pallas_call(kernel, name='soft_moe', out_shape=(jax.ShapeDtypeStruct((...  129 us
    pallas_call x1, Pallas kernels, shards(): pl.pallas_call(token_kernel, name='token_grad', out_shape=(jax.ShapeDtype...  6.28 us

profile of v2, /device:TPU:1, one launch (start us, length us, event | category | flops | bytes accessed | tf_op | source)
XLA Modules:
  0.0 135.9 jit_solution(17010901908193734959)
XLA Ops:
  0.6 129.0 %soft_moe.1 = (f32[16,1280]{1,0:T(8,128)}, bf16[128,1280]{1,0:T(8,128)(2,1)}, bf16[8,16,256]{2,1,0:T(8,128)(2,1)}, bf16[8,16,256]{2,1,0:T(8,128)(2,1)}, bf16[2,3...) custom-call(bf16[8,256,1280]{2,1,0:T(8,128)(2,1)} %tok_h.1, bf16[8,256,1280]{2,1,0:T(8,128)(2,1)} %grad_h.1, ...), custom_call_target="tpu_custom_call" | custom-call | tf_op jit(solution)/shard_map/soft_moe/pallas_call | solution.py:504
  129.6 6.3 %token_grad.1 = (bf16[8,256,1280]{2,1,0:T(8,128)(2,1)}, f32[16,1280]{1,0:T(8,128)}, bf16[2,320,1280]{2,1,0:T(8,128)(2,1)}, bf16[2,320,1280]{2,1,0:T(8,128)(2,1)}) custom-call(bf16[16,1280]{1,0:T(8,128)(2,1)} %bitcast.6, f32[16,1280]{1,0:T(8,128)} %get-tuple-element.14.router_ref, bf16[128,1280]{1,0:T(8,128)(2,1)} %get-tuple-element.15.back_ref, ...), custom_call_target="tpu_custom_call" | custom-call | tf_op jit(solution)/shard_map/token_grad/pallas_call | solution.py:539

commit v3 on v2

--- a/solution.py
+++ b/solution.py
@@ -59,7 +59,11 @@
     return ((r >> 3) & 1) * 64 + (r >> 4) * 8 + (r & 7)
 
 
-X_FIRST = ((0, 1), (1, 0), (1, 1))
+WHOLE, TOP, BOTTOM = (0, 64), (0, 32), (32, 32)
+PIECES = (
+    (((WHOLE, False),), ((WHOLE, True),)),
+    (((TOP, False), (BOTTOM, True)), ((WHOLE, True),)),
+)
 
 
 def rows16(index):
@@ -67,13 +71,13 @@
 
 
 def kernel(
-    tok_h, grad_h, rt_ref, w1_h, w2_h,
-    router_out, back_out, disp_out, lg, dw1_h, dw2_h,
+    tok_h, grad_h, rt_h, w1_h, w2_h,
+    router_out, back_h, disp_h, lg_h, dw1_h, dw2_h,
     tok, grad, w1, w2, disp, comb, stage, a2a_s, a2a_r, rows, parts, rsb,
-    hid, act, act_t, dwk, dws, dwr, fin, back_s, back_r, sb,
-    arp, arr, ars, arg, arf,
+    hid, act, act_t, dwk, dws, dwr, back_s, back_r, sb,
+    arp, arr, ars, arg, arf, rt_v, disp_b, lg,
     s_load, s_w, s_wr, s_a2a, r_a2a, s_ag, r_ag, s_rs, r_rs, s_bk, r_bk,
-    s_dw, r_dw, s_dwo, s_ar, r_ar, s_loc,
+    s_dw, r_dw, s_dwo, s_ar, r_ar, s_loc, s_rt,
 ):
     dp = lax.axis_index("dp")
     ex = lax.axis_index("expert")
@@ -97,6 +101,15 @@
             src_ref=src, dst_ref=dst, send_sem=s_sem, recv_sem=r_sem,
             device_id=device, device_id_type=MESH,
         )
+
+    def load(which, i):
+        src, dst = ((tok_h, tok), (grad_h, grad))[which]
+        return pltpu.make_async_copy(src.at[i], dst.at[i], s_load.at[which, i])
+
+    load_rt = pltpu.make_async_copy(rt_h, rt_v, s_rt.at[0])
+    load_rt.start()
+    for i in range(IMG):
+        load(0, i).start()
 
     barrier = pltpu.get_barrier_semaphore()
     for n in range(1, 16):
@@ -106,14 +119,8 @@
     for k in range(1, 8):
         pl.semaphore_signal(barrier, inc=1, device_id=peer(k), device_id_type=MESH)
 
-    def load(which, i):
-        src, dst = ((tok_h, tok), (grad_h, grad))[which]
-        return pltpu.make_async_copy(src.at[i], dst.at[i], s_load.at[which, i])
-
-    for i in range(IMG):
-        load(0, i).start()
-
-    rt = rt_ref[...]
+    load_rt.wait()
+    rt = rt_v[...]
 
     def pre_in(n, carry):
         for u in range(4):
@@ -128,6 +135,7 @@
             e0 = jnp.exp(logits - jnp.max(logits, axis=0, keepdims=True))
             c = e0 / jnp.sum(e0, axis=0, keepdims=True)
             disp[i] = d
+            disp_b[i] = d.astype(BF)
             comb[i] = c
             stage[rows16(i)] = dot(d.astype(BF), image).astype(BF)
         return carry
@@ -230,7 +238,8 @@
     def to_parts(o, w, j):
         def step(n, carry):
             at = pl.ds(pl.multiple_of(n * 256, 256), 256)
-            parts[o, j, :, at] = dot(act[j], w[j, :, at]).astype(BF)
+            total = dot(act[j], w[j, :, at]).astype(BF)
+            parts[o, j, :, :, at] = total.reshape(8, 64, 256)
             return carry
 
         lax.fori_loop(0, D // 256, step, 0)
@@ -250,63 +259,76 @@
         cp.start()
         dw.append((cp, n, j))
 
-    def rs_copy(o, j, first, count, land, sem, dx, dz):
+    FAR, NEAR = (3, 0), (4, 1)
+
+    def rs_copy(o, j, piece, slot, count, land, sem, dx, dz):
+        at = pl.ds(*piece)
         remote(
-            parts.at[o, j, pl.ds(first, count)], rsb.at[o, j, pl.ds(land, count)],
-            s_rs.at[o, j], r_rs.at[o, j, sem], in_dp(dx, dz),
+            parts.at[o, j, pl.ds(slot, count), at], rsb.at[o, j, pl.ds(land, count), at],
+            s_rs.at[o, j], r_rs.at[o, j, sem + 8 * (piece[0] // 32)], in_dp(dx, dz),
         ).start()
 
-    def part(o, j, first, count):
-        return parts[o, j, pl.ds(first, count)].astype(F32)
-
-    def landed(o, j, land, count, sem):
-        wait_landed(rsb.at[o, j, pl.ds(land, count)], r_rs.at[o, j, sem])
-        return rsb[o, j, pl.ds(land, count)].astype(F32)
+    def part(o, j, piece, slot, count=1):
+        return parts[o, j, pl.ds(slot, count), pl.ds(*piece)].astype(F32)
+
+    def landed(o, j, piece, land, count, sem):
+        ref = rsb.at[o, j, pl.ds(land, count), pl.ds(*piece)]
+        wait_landed(ref, r_rs.at[o, j, sem + 8 * (piece[0] // 32)])
+        return ref[...].astype(F32)
 
     def rs_begin(o, j):
-        if (o, j) in X_FIRST:
-            rs_copy(o, j, 256, 128, 0, 0, 3, 0)
-            rs_copy(o, j, 384, 128, 128, 1, 1, 0)
-        else:
-            for dx in (2, 1, 3, 0):
-                rs_copy(o, j, 128 * dx + 64, 64, 64 * dx, 3 + dx, 0, 1)
-
-    def rs_add(o, j, dx):
-        total = part(o, j, 128 * dx, 64) + landed(o, j, 64 * dx, 64, 3 + dx)
-        parts[o, j, pl.ds(128 * dx, 64)] = total.astype(BF)
-
-    def rs_far(o, j):
-        rs_add(o, j, 2)
-        rs_copy(o, j, 256, 64, 256, 0, 3, 0)
-
-    def rs_near(o, j):
-        rs_add(o, j, 3)
-        rs_copy(o, j, 384, 64, 320, 1, 1, 0)
-        rs_add(o, j, 1)
-
-    def rs_second(o, j):
-        if (o, j) in X_FIRST:
-            count, land, last = 128, 0, 256
-        else:
-            count, land, last = 64, 256, 384
-        total = part(o, j, 128, count) + landed(o, j, land, count, 0)
-        parts[o, j, pl.ds(128, count)] = total.astype(BF)
-        rs_copy(o, j, 128, count, last, 1, 3, 0)
-
-    def rs_third(o, j):
-        both = landed(o, j, 128, 256, 1)
-        total = part(o, j, 64, 64) + both[64:128] + both[192:256]
-        parts[o, j, pl.ds(64, 64)] = total.astype(BF)
-        rs_copy(o, j, 64, 64, 384, 2, 0, 1)
-        fin[pl.ds(64 * j, 64)] = (part(o, j, 0, 64) + both[:64] + both[128:192])
+        for piece, x_first in PIECES[o][j]:
+            if x_first:
+                for dz in (1, 0):
+                    rs_copy(o, j, piece, 4 + dz, 1, dz, FAR[dz], 3, 0)
+                for dz in (1, 0):
+                    rs_copy(o, j, piece, 6 + dz, 1, 2 + dz, NEAR[dz], 1, 0)
+            else:
+                for dx in (2, 3, 1, 0):
+                    rs_copy(o, j, piece, 2 * dx + 1, 1, dx, 3 + dx, 0, 1)
+
+    def rs_add(o, j, piece, dx):
+        total = part(o, j, piece, 2 * dx) + landed(o, j, piece, dx, 1, 3 + dx)
+        parts[o, j, pl.ds(2 * dx, 1), pl.ds(*piece)] = total.astype(BF)
+
+    def rs_far(o, j, piece):
+        rs_add(o, j, piece, 2)
+        rs_copy(o, j, piece, 4, 1, 4, 0, 3, 0)
+
+    def rs_near(o, j, piece):
+        rs_add(o, j, piece, 3)
+        rs_copy(o, j, piece, 6, 1, 5, 1, 1, 0)
+        rs_add(o, j, piece, 1)
+
+    def rs_second(o, j, which=0):
+        piece, x_first = PIECES[o][j][which]
+        for slot, land, sem, last, last_sem in (
+            ((3, 1, FAR[1], 5, NEAR[1]), (2, 0, FAR[0], 4, NEAR[0])) if x_first
+            else ((2, 4, 0, 6, 1),)
+        ):
+            total = part(o, j, piece, slot) + landed(o, j, piece, land, 1, sem)
+            parts[o, j, pl.ds(slot, 1), pl.ds(*piece)] = total.astype(BF)
+            rs_copy(o, j, piece, slot, 1, last, last_sem, 3, 0)
+
+    def ring_total(o, j, piece, dz):
+        at = pl.ds(*piece)
+        wait_landed(rsb.at[o, j, pl.ds(2, 2), at], r_rs.at[o, j, NEAR[dz] + 8 * (piece[0] // 32)])
+        right, left = rsb[o, j, 2 + dz, at], rsb[o, j, 4 + dz, at]
+        return part(o, j, piece, dz)[0] + right.astype(F32) + left.astype(F32)
+
+    def rs_third(o, j, which=0):
+        piece = PIECES[o][j][which][0]
+        parts[o, j, 1, pl.ds(*piece)] = ring_total(o, j, piece, 1).astype(BF)
+        rs_copy(o, j, piece, 1, 1, 6, 2, 0, 1)
 
     def rs_end(o, j):
-        if (o, j) in X_FIRST:
-            total = fin[pl.ds(64 * j, 64)] + landed(o, j, 384, 64, 2)
-        else:
-            both = landed(o, j, 320, 128, 1)
-            total = part(o, j, 0, 64) + both[:64] + both[64:] + landed(o, j, 0, 64, 3)
-        back_s[o, pl.ds(64 * j, 64)] = total.astype(BF)
+        for piece, x_first in PIECES[o][j]:
+            if x_first:
+                total = ring_total(o, j, piece, 0) + landed(o, j, piece, 6, 1, 2)[0]
+            else:
+                both = landed(o, j, piece, 5, 2, 1)
+                total = part(o, j, piece, 0)[0] + both[0] + both[1] + landed(o, j, piece, 0, 1, 3)[0]
+            back_s[o, pl.ds(64 * j + piece[0], piece[1])] = total.astype(BF)
 
     def give_back(o):
         back_s[o] = permute_rows(by_peer, back_s[o])
@@ -354,8 +376,8 @@
         cp.wait()
     for cp in far_w:
         cp.wait_recv()
+    ag_second(1)
     hidden_step(0)
-    ag_second(1)
     to_parts(0, w2, 0)
     rs_begin(0, 0)
     hidden_step(1)
@@ -365,23 +387,29 @@
     grad_step(0)
     rs_second(0, 1)
     grad_step(1)
-    rs_far(0, 0)
-    rs_near(0, 0)
     weight_grad(1, 1, 0)
-    rs_third(0, 1)
-    rs_second(1, 0)
-    rs_second(0, 0)
     weight_grad(1, 1, 1)
-    rs_second(1, 1)
-    rs_third(1, 0)
-    rs_end(0, 0)
-    rs_end(0, 1)
-    give_back(0)
     act_t[0] = act[0].T
     weight_grad(0, 0, 0)
-    rs_third(1, 1)
+    rs_second(1, 0, 1)
+    rs_far(0, 0, WHOLE)
+    rs_near(0, 0, WHOLE)
+    rs_third(0, 1)
+    rs_second(1, 1)
+    rs_second(0, 0)
+    rs_far(1, 0, TOP)
     act_t[1] = act[1].T
     weight_grad(0, 0, 1)
+    rs_near(1, 0, TOP)
+    rs_third(1, 0, 1)
+    rs_second(1, 0, 0)
+    rs_end(0, 1)
+    rs_third(1, 1)
+    rs_end(0, 0)
+    give_back(0)
+    rs_end(1, 0)
+    rs_end(1, 1)
+    give_back(1)
     sb[0] = take_back(0)
 
     def comb_side(n, carry):
@@ -394,20 +422,12 @@
 
     lax.fori_loop(0, IMG // 4, comb_side, 0)
 
-    rs_end(1, 0)
-    rs_end(1, 1)
-    give_back(1)
-
-    for cp, n, j in dw:
-        cp.wait()
-        dws[n, j] = (dwk[n, j] + dwr[n, j].astype(F32)).astype(BF)
-        out = (dw1_h, dw2_h)[n]
-        pltpu.make_async_copy(dws.at[n, j], out.at[j], s_dwo.at[n, j]).start()
-
     sb[1] = take_back(1)
-    back_out[...] = sb[1]
-    for i in range(IMG):
-        disp_out[i] = disp[i].astype(BF)
+    small = [
+        pltpu.make_async_copy(sb.at[1], back_h, s_rt.at[0]),
+        pltpu.make_async_copy(disp_b, disp_h, s_rt.at[1]),
+        pltpu.make_async_copy(lg, lg_h, s_rt.at[2]),
+    ]
 
     def disp_side(n, total):
         for u in range(4):
@@ -430,6 +450,8 @@
 
     for k in range(1, 8):
         remote(arp.at[ex_of(k)], arr.at[k], s_ar.at[0], r_ar.at[0], peer(k)).start()
+    for cp in small:
+        cp.start()
     for n in range(2):
         wait_sent(a2a_s.at[n, pl.ds(0, 112)], s_a2a.at[n])
         wait_sent(back_s.at[n, pl.ds(0, 112)], s_bk.at[n])
@@ -448,10 +470,13 @@
     arg[dp] = total
     for cp in far_w:
         cp.wait_send()
-    for n in range(2):
-        for j in range(2):
-            out = (dw1_h, dw2_h)[n]
-            pltpu.make_async_copy(dws.at[n, j], out.at[j], s_dwo.at[n, j]).wait()
+
+    for cp, n, j in dw:
+        cp.wait()
+        dws[n, j] = (dwk[n, j] + dwr[n, j].astype(F32)).astype(BF)
+        out = (dw1_h, dw2_h)[n]
+        pltpu.make_async_copy(dws.at[n, j], out.at[j], s_dwo.at[n, j]).start()
+
     wait_landed(arg.at[pl.ds(0, 15)], r_ar.at[1])
     total = arg[0]
     for n in range(1, 16):
@@ -462,6 +487,12 @@
     arf[ex] = total
     wait_sent(arp.at[pl.ds(0, 7)], s_ar.at[0])
     wait_sent(arg.at[pl.ds(0, 15)], s_ar.at[1])
+    for cp in small:
+        cp.wait()
+    for n in range(2):
+        for j in range(2):
+            out = (dw1_h, dw2_h)[n]
+            pltpu.make_async_copy(dws.at[n, j], out.at[j], s_dwo.at[n, j]).wait()
     wait_landed(arf.at[pl.ds(0, 7)], r_ar.at[2])
     for p in range(8):
         lane = 384 * (p // 2)
@@ -471,27 +502,36 @@
 
 
 def token_kernel(
-    rt_ref, router_ref, back_ref, disp_ref, lg_ref, dw1_in, dw2_in,
-    token_grad_h, router_out, dw1_h, dw2_h, tgo, dwv, s_out, s_in, s_dw,
+    rt_h, router_h, back_h, disp_h, lg_h, dw1_in, dw2_in,
+    token_grad_h, router_out, dw1_h, dw2_h,
+    rt_v, router_v, back_v, disp_v, lg_v, tgo, dwv, s_small, s_out, s_in, s_dw,
 ):
+    small = [
+        pltpu.make_async_copy(src, dst, s_small.at[n])
+        for n, (src, dst) in enumerate((
+            (rt_h, rt_v), (back_h, back_v), (disp_h, disp_v), (lg_h, lg_v), (router_h, router_v)))
+    ]
     reads, writes = [], []
     for n, (src, dst) in enumerate(((dw1_in, dw1_h), (dw2_in, dw2_h))):
         reads.append(pltpu.make_async_copy(src, dwv.at[n], s_in.at[n]))
         writes.append(pltpu.make_async_copy(dwv.at[n], dst, s_dw.at[n]))
-    for cp in reads:
+    router_write = pltpu.make_async_copy(router_v, router_out, s_small.at[5])
+    for cp in small + reads:
         cp.start()
-    router_out[...] = router_ref[...]
+    for cp in small:
+        cp.wait()
+    router_write.start()
     for i in range(IMG):
-        left = jnp.concatenate([disp_ref[i], lg_ref[i]], axis=0)
-        right = jnp.concatenate([back_ref[pl.ds(i * 16, 16)], rt_ref[...]], axis=0)
+        left = jnp.concatenate([disp_v[i], lg_v[i]], axis=0)
+        right = jnp.concatenate([back_v[pl.ds(i * 16, 16)], rt_v[...]], axis=0)
         tgo[i] = dot_tn(left, right).astype(BF)
         cp = pltpu.make_async_copy(tgo.at[i], token_grad_h.at[i], s_out.at[i])
         cp.start()
         writes.append(cp)
-        if i in (2, 4):
-            reads[i // 2 - 1].wait()
-            writes[i // 2 - 1].start()
-    for cp in writes:
+        if i in (1, 3):
+            reads[i // 2].wait()
+            writes[i // 2].start()
+    for cp in writes + [router_write]:
         cp.wait()
 
 
@@ -512,25 +552,26 @@
             jax.ShapeDtypeStruct((2, HID, D), BF),
             jax.ShapeDtypeStruct((2, HID, D), BF),
         ),
-        in_specs=[any_space, any_space, vmem, any_space, any_space],
-        out_specs=(vmem, vmem, vmem, vmem, any_space, any_space),
+        in_specs=[any_space] * 5,
+        out_specs=(vmem,) + (any_space,) * 5,
         scratch_shapes=[
             V((IMG, M, D), BF), V((IMG, M, D), BF),
             V((2, HID2, D), BF), V((2, HID2, D), BF),
             V((IMG, S, M), F32), V((IMG, S, M), F32),
             V((128, D), BF), V((2, 128, D), BF), V((2, 128, D), BF),
-            V((2, 2, ROWS, D), BF), V((2, 2, ROWS, D), BF),
-            V((2, 2, 448, D), BF),
+            V((2, 2, ROWS, D), BF), V((2, 2, 8, 64, D), BF),
+            V((2, 2, 7, 64, D), BF),
             V((2, ROWS, HID2), F32), V((2, ROWS, HID2), BF), V((2, HID2, ROWS), BF),
             V((2, 2, HID, D), F32), V((2, 2, HID, D), BF), V((2, 2, HID, D), BF),
-            V((128, D), F32), V((2, 128, D), BF), V((2, 128, D), BF),
+            V((2, 128, D), BF), V((2, 128, D), BF),
             V((2, 128, D), BF),
             V((8, 8, 384), F32), V((8, 8, 384), F32), V((2, 8, 384), F32),
             V((16, 8, 384), F32), V((8, 8, 384), F32),
+            V((S, D), BF), V((IMG, S, M), BF), V((IMG, S, M), BF),
             dma((2, IMG)), dma((2, 2)), dma((2, 2)), dma((2,)), dma((2,)),
-            dma((2, 2)), dma((2, 2, 8)), dma((2, 2)), dma((2, 2, 8)),
+            dma((2, 2)), dma((2, 2, 8)), dma((2, 2)), dma((2, 2, 16)),
             dma((2,)), dma((2,)), dma((2, 2)), dma((2, 2)), dma((2, 2)),
-            dma((3,)), dma((3,)), dma((2, 2)),
+            dma((3,)), dma((3,)), dma((2, 2)), dma((3,)),
         ],
         compiler_params=pltpu.CompilerParams(
             collective_id=0, has_side_effects=True, vmem_limit_bytes=62 * 2**20
@@ -545,10 +586,11 @@
             jax.ShapeDtypeStruct((2, HID, D), BF),
             jax.ShapeDtypeStruct((2, HID, D), BF),
         ),
-        in_specs=[vmem] * 5 + [any_space] * 2,
-        out_specs=(any_space, vmem, any_space, any_space),
+        in_specs=[any_space] * 7,
+        out_specs=(any_space,) * 4,
         scratch_shapes=[
-            V((IMG, M, D), BF), V((2, 2, HID, D), BF), dma((IMG,)), dma((2,)), dma((2,)),
+            V((S, D), BF), V((S, D), F32), V((128, D), BF), V((IMG, S, M), BF), V((IMG, S, M), BF),
+            V((IMG, M, D), BF), V((2, 2, HID, D), BF), dma((6,)), dma((IMG,)), dma((2,)), dma((2,)),
         ],
         compiler_params=pltpu.CompilerParams(vmem_limit_bytes=62 * 2**20),
     )(router_t, router_grad, back, disp_half, grad_logit, dw1, dw2)

time: 136 us -> 130 us (0.956)
  Pallas kernels: 135 us -> 129 us
    pallas_call x1, Pallas kernels: 129 us -> 123 us  [shards(): pl.pallas_call(kernel, name='soft_moe', out_shape=(jax.ShapeDtypeStruct((...]
where the time goes in v3:
time: 130 us; the launch traced here: 129 us
  Pallas kernels  129 us (99%)
    pallas_call x1, Pallas kernels, shards(): pl.pallas_call(kernel, name='soft_moe', out_shape=(jax.ShapeDtypeStruct((...  123 us
    pallas_call x1, Pallas kernels, shards(): pl.pallas_call(token_kernel, name='token_grad', out_shape=(jax.ShapeDtype...  5.43 us

profile of v3, /device:TPU:1, one launch (start us, length us, event | category | flops | bytes accessed | tf_op | source)
XLA Modules:
  0.0 129.5 jit_solution(421822885217564692)
XLA Ops:
  0.6 123.3 %soft_moe.1 = (f32[16,1280]{1,0:T(8,128)}, bf16[128,1280]{1,0:T(8,128)(2,1)}, bf16[8,16,256]{2,1,0:T(8,128)(2,1)}, bf16[8,16,256]{2,1,0:T(8,128)(2,1)}, bf16[2,3...) custom-call(bf16[8,256,1280]{2,1,0:T(8,128)(2,1)} %tok_h.1, bf16[8,256,1280]{2,1,0:T(8,128)(2,1)} %grad_h.1, ...), custom_call_target="tpu_custom_call" | custom-call | tf_op jit(solution)/shard_map/soft_moe/pallas_call | solution.py:544
  123.9 5.4 %token_grad.1 = (bf16[8,256,1280]{2,1,0:T(8,128)(2,1)}, f32[16,1280]{1,0:T(8,128)}, bf16[2,320,1280]{2,1,0:T(8,128)(2,1)}, bf16[2,320,1280]{2,1,0:T(8,128)(2,1)}) custom-call(bf16[16,1280]{1,0:T(8,128)(2,1)} %bitcast.6, f32[16,1280]{1,0:T(8,128)} %get-tuple-element.14.router_h, bf16[128,1280]{1,0:T(8,128)(2,1)} %get-tuple-element.15.back_h, ...), custom_call_target="tpu_custom_call" | custom-call | tf_op jit(solution)/shard_map/token_grad/pallas_call | solution.py:580

commit v4 on v3

--- a/solution.py
+++ b/solution.py
@@ -213,32 +213,31 @@
     def ag_end(a, j):
         wait_landed(rows.at[a, j, pl.ds(256, 256)], r_ag.at[a, j, 0])
 
-    def project(a, w, j, finish):
+    def project_in(j):
         for h in range(2):
-            hid[j, pl.ds(h * 256, 256)] = finish(
-                j, h, dot_nt(rows[a, j, pl.ds(h * 256, 256)], w[j]))
-
-    def keep(j, h, value):
-        return value
+            at = pl.ds(h * 256, 256)
+            hid[j, at] = dot_nt(rows[0, j, at], w1[j])
+
+    def project_grad(j):
+        for h in range(2):
+            at = pl.ds(h * 256, 256)
+            act[1, j, at] = (dot_nt(rows[1, j, at], w2[j]) * hid[j, at]).astype(BF)
 
     def gelu(j):
         def step(n, carry):
             at = pl.ds(pl.multiple_of(n * 32, 32), 32)
             v = hid[j, at]
             half = 0.5 * (1.0 + lax.erf(v * root_half))
-            act[j, at] = (v * half).astype(BF)
+            act[0, j, at] = (v * half).astype(BF)
             hid[j, at] = half + v * jnp.exp(-0.5 * v * v) * inv_root_tau
             return carry
 
         lax.fori_loop(0, ROWS // 32, step, 0)
-
-    def slope(j, h, value):
-        return value * hid[j, pl.ds(h * 256, 256)]
 
     def to_parts(o, w, j):
         def step(n, carry):
             at = pl.ds(pl.multiple_of(n * 256, 256), 256)
-            total = dot(act[j], w[j, :, at]).astype(BF)
+            total = dot(act[o, j], w[j, :, at]).astype(BF)
             parts[o, j, :, :, at] = total.reshape(8, 64, 256)
             return carry
 
@@ -246,10 +245,12 @@
 
     dw = []
 
-    def weight_grad(n, a, j):
+    def weight_grad(n, j):
+        act_t[...] = act[1 - n, j].T
+
         def step(m, carry):
             at = pl.ds(pl.multiple_of(m * 256, 256), 256)
-            total = dot(act_t[j], rows[a, j, :, at])
+            total = dot(act_t[...], rows[n, j, :, at])
             dwk[n, j, :, at] = total[:HID]
             dws[n, j, :, at] = total[HID:].astype(BF)
             return carry
@@ -345,14 +346,12 @@
 
     def hidden_step(j):
         ag_end(0, j)
-        project(0, w1, j, keep)
+        project_in(j)
         gelu(j)
 
     def grad_step(j):
         ag_end(1, j)
-        project(1, w2, j, slope)
-        act_t[j] = act[j].T
-        act[j] = hid[j].astype(BF)
+        project_grad(j)
         to_parts(1, w1, j)
         rs_begin(1, j)
 
@@ -387,10 +386,9 @@
     grad_step(0)
     rs_second(0, 1)
     grad_step(1)
-    weight_grad(1, 1, 0)
-    weight_grad(1, 1, 1)
-    act_t[0] = act[0].T
-    weight_grad(0, 0, 0)
+    weight_grad(1, 0)
+    weight_grad(1, 1)
+    weight_grad(0, 0)
     rs_second(1, 0, 1)
     rs_far(0, 0, WHOLE)
     rs_near(0, 0, WHOLE)
@@ -398,8 +396,7 @@
     rs_second(1, 1)
     rs_second(0, 0)
     rs_far(1, 0, TOP)
-    act_t[1] = act[1].T
-    weight_grad(0, 0, 1)
+    weight_grad(0, 1)
     rs_near(1, 0, TOP)
     rs_third(1, 0, 1)
     rs_second(1, 0, 0)
@@ -561,7 +558,7 @@
             V((128, D), BF), V((2, 128, D), BF), V((2, 128, D), BF),
             V((2, 2, ROWS, D), BF), V((2, 2, 8, 64, D), BF),
             V((2, 2, 7, 64, D), BF),
-            V((2, ROWS, HID2), F32), V((2, ROWS, HID2), BF), V((2, HID2, ROWS), BF),
+            V((2, ROWS, HID2), F32), V((2, 2, ROWS, HID2), BF), V((HID2, ROWS), BF),
             V((2, 2, HID, D), F32), V((2, 2, HID, D), BF), V((2, 2, HID, D), BF),
             V((2, 128, D), BF), V((2, 128, D), BF),
             V((2, 128, D), BF),

time: 130 us -> 130 us (level)
  no operation moved by 1% of the time
where the time goes in v4:
time: 130 us
  Pallas kernels  129 us (99%)
    pallas_call x1, Pallas kernels, shards(): pl.pallas_call(kernel, name='soft_moe', out_shape=(jax.ShapeDtypeStruct((...  123 us
    pallas_call x1, Pallas kernels, shards(): pl.pallas_call(token_kernel, name='token_grad', out_shape=(jax.ShapeDtype...  5.43 us

profile of v4, /device:TPU:1, one launch (start us, length us, event | category | flops | bytes accessed | tf_op | source)
XLA Modules:
  0.0 129.7 jit_solution(2215727095152036880)
XLA Ops:
  0.6 123.5 %soft_moe.1 = (f32[16,1280]{1,0:T(8,128)}, bf16[128,1280]{1,0:T(8,128)(2,1)}, bf16[8,16,256]{2,1,0:T(8,128)(2,1)}, bf16[8,16,256]{2,1,0:T(8,128)(2,1)}, bf16[2,3...) custom-call(bf16[8,256,1280]{2,1,0:T(8,128)(2,1)} %tok_h.1, bf16[8,256,1280]{2,1,0:T(8,128)(2,1)} %grad_h.1, ...), custom_call_target="tpu_custom_call" | custom-call | tf_op jit(solution)/shard_map/soft_moe/pallas_call | solution.py:541
  124.1 5.4 %token_grad.1 = (bf16[8,256,1280]{2,1,0:T(8,128)(2,1)}, f32[16,1280]{1,0:T(8,128)}, bf16[2,320,1280]{2,1,0:T(8,128)(2,1)}, bf16[2,320,1280]{2,1,0:T(8,128)(2,1)}) custom-call(bf16[16,1280]{1,0:T(8,128)(2,1)} %bitcast.6, f32[16,1280]{1,0:T(8,128)} %get-tuple-element.14.router_h, bf16[128,1280]{1,0:T(8,128)(2,1)} %get-tuple-element.15.back_h, ...), custom_call_target="tpu_custom_call" | custom-call | tf_op jit(solution)/shard_map/token_grad/pallas_call | solution.py:577
